TPU v7x, 32 devices: a whole 2x2x4 slice. The times are simulated.
32 devices in a mesh: freq: 2 (over x), row: 16 (over z, y, core).
Axes of the slice: x: 2, y: 2, z: 4, core: 2. Of those that a mesh axis runs over, the one named last changes fastest.
Arguments:
- data_real: bfloat16 [16384, 8192], P(('freq', 'row')), parts along dimension 0, may hold values from -6 to 6
- data_imag: bfloat16 [16384, 8192], P(('freq', 'row')), parts along dimension 0, may hold values from -6 to 6
- counts: int32 [8, 8], replicated, may hold values from 0 to 4
- source_cols: int32 [128], replicated, may hold values from 0 to 8191, as said below
Outputs:
- pred_real: float32 [16384, 128], P(('freq', 'row')), parts along dimension 0
- pred_imag: float32 [16384, 128], P(('freq', 'row')), parts along dimension 0
There are 2 independent parts, one for each index of `freq`. A program takes and returns all parts, laid end to end along the dimension named above; an argument that names none is the same for every part. Nothing has to cross between parts.
Inputs may be any that keep to these rules, and one draw needn't show every extreme that they name: `source_cols`: 128 distinct grid points; 0 and 8191 are always among them.
All inputs are finite; a program needn't handle non-finite values.
Results may differ from a plain program's by a relative error of at most 0.0029.
Values may be sent and summed in bfloat16 or wider, within the bound.
No kernel may reach another device: no remote copies, remote signals or barrier semaphores. Data moves between devices by JAX's collectives and lax.ppermute only.
A program may use at most 128 MiB of HBM per device.

v0:
```python
import functools
import math

import jax
import jax.numpy as jnp
from jax import lax
from jax.experimental import pallas as pl
from jax.experimental.pallas import tpu as pltpu
from jax.sharding import PartitionSpec as P

TILES = 8
AXIS = "row"
CORE, Y, LOW, HIGH = 1, 2, 4, 8
GROUP = 16
MIRROR_COST = 10000000000
DIRECT_COST = 2000000000
PIECE = 1024
F32 = jnp.float32
BF16 = jnp.bfloat16


def params(mib=16):
    return pltpu.CompilerParams(vmem_limit_bytes=mib * 1024 * 1024)


def whole_vmem():
    return pl.BlockSpec(memory_space=pltpu.VMEM)


def anywhere():
    return pl.BlockSpec(memory_space=pl.ANY)


def in_hbm(value):
    return pltpu.with_memory_space_constraint(value, pltpu.HBM)


def whole_smem():
    return pl.BlockSpec(memory_space=pltpu.SMEM)


def cost(flops, size):
    return pl.CostEstimate(flops=flops, bytes_accessed=size, transcendentals=0)


def dot(left, right):
    return jnp.dot(left, right, preferred_element_type=F32)


def ranks_of(col, rows):
    count = col.shape[0]
    owner = col // rows
    owner_row = jnp.transpose(jnp.broadcast_to(owner.astype(F32), (count, count))).astype(jnp.int32)
    before = lax.broadcasted_iota(jnp.int32, (count, count), 1) < lax.broadcasted_iota(
        jnp.int32, (count, count), 0
    )
    same = (owner_row == owner) & before
    return jnp.sum(same.astype(F32), axis=1, keepdims=True).astype(jnp.int32)


def rows_kernel(cap, round_ref, me_ref, col_ref, real_ref, imag_ref, out_ref, list_ref, near_ref, held_ref, sems):
    rows, width = real_ref.shape
    groups = out_ref.shape[0]
    count = col_ref.shape[0]
    base = me_ref[0] * rows
    skip = round_ref[0] * cap

    def copies(slot, local):
        group = pl.ds(pl.multiple_of(local // GROUP * GROUP, GROUP), GROUP)
        return [
            pltpu.make_async_copy(ref.at[group], near_ref.at[slot, part], sems.at[slot, part])
            for part, ref in enumerate((real_ref, imag_ref))
        ]

    def begin(s, found):
        local = col_ref[s] - base
        own = (local >= 0) & (local < rows)
        slot = found - skip

        @pl.when(own & (slot >= 0) & (slot < cap))
        def _():
            list_ref[slot] = local
            for copy in copies(slot, local):
                copy.start()

        return found + own.astype(jnp.int32)

    def pick(slot, _):
        local = list_ref[slot]
        chosen = lax.broadcasted_iota(jnp.int32, (GROUP, PIECE), 0) == local % GROUP
        for part, copy in enumerate(copies(slot, local)):
            copy.wait()
            for at in range(0, width, PIECE):
                group = near_ref[slot, part, :, at : at + PIECE].astype(F32)
                held_ref[pl.ds(part * cap + slot, 1), at : at + PIECE] = jnp.sum(
                    jnp.where(chosen, group, 0.0), axis=0, keepdims=True
                )
        return 0

    found = lax.fori_loop(0, count, begin, jnp.int32(0))
    held_ref[...] = jnp.zeros_like(held_ref)
    lax.fori_loop(0, jnp.clip(found - skip, 0, cap), pick, 0)
    for g in range(groups):
        out_ref[g] = held_ref[:, g * rows : (g + 1) * rows].astype(BF16)


def own_source_rows(me, data_real, data_imag, source_cols, which, cap):
    rows, width = data_real.shape
    return pl.pallas_call(
        functools.partial(rows_kernel, cap),
        in_specs=[whole_smem()] * 3 + [anywhere()] * 2,
        out_specs=whole_vmem(),
        out_shape=jax.ShapeDtypeStruct((width // rows, 2 * cap, rows), BF16),
        scratch_shapes=[
            pltpu.SMEM((cap,), jnp.int32),
            pltpu.VMEM((cap, 2, GROUP, width), BF16),
            pltpu.VMEM((2 * cap, width), F32),
            pltpu.SemaphoreType.DMA((cap, 2)),
        ],
        compiler_params=params(24),
        cost_estimate=cost(0, 2 * cap * width),
        name="own_source_rows",
    )(which, me, source_cols, data_real, data_imag)


def cols_kernel(real_ref, imag_ref, row_ref, out_ref, acc_ref):
    rows, step = real_ref.shape
    count = row_ref.shape[1]
    t = pl.program_id(0)

    @pl.when(t == 0)
    def _():
        acc_ref[...] = jnp.zeros_like(acc_ref)

    place = lax.broadcasted_iota(jnp.int32, (step, count), 0) + t * step
    pick = (place == row_ref[...]).astype(F32).astype(BF16)
    acc_ref[:, :count] += dot(real_ref[...], pick)
    acc_ref[:, count:] += dot(imag_ref[...], pick)

    @pl.when(t == pl.num_programs(0) - 1)
    def _():
        out_ref[...] = jnp.transpose(acc_ref[...]).astype(BF16)


def own_source_cols(data_real, data_imag, row, step):
    rows, width = data_real.shape
    count = row.shape[1]
    block = pl.BlockSpec((rows, step), lambda t: (0, t))
    return pl.pallas_call(
        cols_kernel,
        grid=(width // step,),
        in_specs=[block, block, whole_vmem()],
        out_specs=pl.BlockSpec((2 * count, rows), lambda t: (0, 0)),
        out_shape=jax.ShapeDtypeStruct((2 * count, rows), BF16),
        scratch_shapes=[pltpu.VMEM((rows, 2 * count), F32)],
        compiler_params=params(),
        cost_estimate=cost(4 * rows * width * count, 4 * rows * width),
        name="own_source_cols",
    )(data_real, data_imag, row)


def select_kernel(cap, round_ref, got_ref, col_ref, out_ref):
    out_ref[...] = pick_rows(cap, round_ref[0], got_ref, col_ref).astype(BF16)


def select_rows(got, col, which, cap):
    groups, _, rows = got.shape
    count = col.shape[0]
    return pl.pallas_call(
        functools.partial(select_kernel, cap),
        in_specs=[whole_smem(), whole_vmem(), whole_vmem()],
        out_specs=whole_vmem(),
        out_shape=jax.ShapeDtypeStruct((2 * count, rows), BF16),
        compiler_params=params(),
        cost_estimate=cost(8 * count * groups * cap * rows, 4 * groups * cap * rows),
        name="select_rows",
    )(which, got, col)


def pick_rows(cap, which, got_ref, col_ref):
    groups, _, rows = got_ref.shape
    count = col_ref.shape[0]
    col = col_ref[...]
    slot = ranks_of(col, rows) - which * cap
    inside = (slot >= 0) & (slot < cap)
    place = jnp.where(inside, (col // rows) * (2 * cap) + slot, -1)
    lanes = lax.broadcasted_iota(jnp.int32, (count, groups * 2 * cap), 1)
    pick = jnp.concatenate([lanes == place, lanes == jnp.where(inside, place + cap, -1)], axis=0)
    got = got_ref[...].reshape(groups * 2 * cap, rows)
    return dot(pick.astype(F32).astype(BF16), got)


def own_panel(width, mine, counts_ref, rowpart_ref, colpart_ref, col_ref):
    tile = width // TILES
    tiles = col_ref[...] // tile
    forward = jnp.zeros_like(tiles)
    backward = jnp.zeros_like(tiles)
    for t in range(TILES):
        forward = jnp.where(tiles == t, counts_ref[mine, t], forward)
        backward = jnp.where(tiles == t, counts_ref[t, mine], backward)
    forward = jnp.concatenate([forward, forward], axis=0).astype(F32)
    backward = jnp.concatenate([backward, backward], axis=0).astype(F32)
    own = colpart_ref[...].astype(F32)
    mirror = rowpart_ref[...].astype(F32)
    return (forward * own + backward * mirror) / jnp.maximum(forward + backward, 1.0)


def store_panel(panel, panel_ref, panel_t_ref):
    double, rows = panel.shape
    count = double // 2
    panel_t_ref[:, :rows] = panel.astype(BF16)
    panel_t_ref[:count, rows:] = (-panel[count:]).astype(BF16)
    panel_t_ref[count:, rows:] = panel[:count].astype(BF16)
    panel_ref[...] = jnp.transpose(panel).astype(BF16)


def panel_kernel(
    width, me_ref, counts_ref, rowpart_ref, colpart_ref, col_ref, panel_ref, panel_t_ref
):
    mine = me_ref[0] * rowpart_ref.shape[1] // (width // TILES)
    panel = own_panel(width, mine, counts_ref, rowpart_ref, colpart_ref, col_ref)
    store_panel(panel, panel_ref, panel_t_ref)


def panel_only(me, counts, rowpart, colpart, col, width):
    double, rows = colpart.shape
    return pl.pallas_call(
        functools.partial(panel_kernel, width),
        in_specs=[whole_smem()] * 2 + [whole_vmem()] * 3,
        out_specs=[whole_vmem()] * 2,
        out_shape=[
            jax.ShapeDtypeStruct((rows, double), BF16),
            jax.ShapeDtypeStruct((double, 2 * rows), BF16),
        ],
        compiler_params=params(),
        cost_estimate=cost(8 * rows * double, 8 * rows * double),
        name="panel_only",
    )(me, counts, rowpart, colpart, col)


def weight(counts_ref, mine, other, shape):
    forward = jnp.full(shape, counts_ref[mine, other], jnp.int32).astype(F32)
    backward = jnp.full(shape, counts_ref[other, mine], jnp.int32).astype(F32)
    return forward / jnp.maximum(forward + backward, 1.0)


def mirror_block(real, imag, panel_t):
    rows = real.shape[0]
    return dot(panel_t[:, :rows], real) + dot(panel_t[:, rows:], imag)


def direct_block(real, imag, panel):
    count = panel.shape[1] // 2
    turned = jnp.concatenate([-panel[:, count:], panel[:, :count]], axis=1)
    return dot(real, panel) + dot(imag, turned)


def mirror_kernel(width, me_ref, counts_ref, real_ref, imag_ref, panel_t_ref, out_ref):
    rows, tile = real_ref.shape
    mine = me_ref[0] * rows // tile
    found = mirror_block(real_ref[...], imag_ref[...], panel_t_ref[...])
    found = found * weight(counts_ref, mine, pl.program_id(0), (1, tile))
    for g in range(out_ref.shape[0]):
        out_ref[g] = found[:, g * rows : (g + 1) * rows]


def mirror_term(me, counts, data_real, data_imag, panel_t):
    rows, width = data_real.shape
    double = panel_t.shape[0]
    tile = width // TILES
    block = pl.BlockSpec((rows, tile), lambda t: (0, t))
    return pl.pallas_call(
        functools.partial(mirror_kernel, width),
        grid=(TILES,),
        in_specs=[whole_smem()] * 2 + [block, block, whole_vmem()],
        out_specs=pl.BlockSpec((tile // rows, double, rows), lambda t: (t, 0, 0)),
        out_shape=jax.ShapeDtypeStruct((width // rows, double, rows), F32),
        compiler_params=params(32),
        cost_estimate=cost(4 * rows * width * double, 4 * rows * width + 2 * double * width),
        name="mirror_term",
    )(me, counts, data_real, data_imag, panel_t)


def direct_kernel(width, me_ref, counts_ref, real_ref, imag_ref, panel_ref, out_ref):
    rows, tile = real_ref.shape
    mine = me_ref[0] * rows // tile
    t = pl.program_id(0)

    @pl.when(t == 0)
    def _():
        out_ref[...] = jnp.zeros_like(out_ref)

    found = direct_block(real_ref[...], imag_ref[...], panel_ref[...])
    out_ref[...] += found * weight(counts_ref, mine, t, (1, out_ref.shape[1]))


def direct_term(me, counts, data_real, data_imag, panel):
    rows, width = data_real.shape
    double = panel.shape[1]
    tile = width // TILES
    block = pl.BlockSpec((rows, tile), lambda t: (0, t))
    return pl.pallas_call(
        functools.partial(direct_kernel, width),
        grid=(TILES,),
        in_specs=[whole_smem()] * 2 + [block, block, pl.BlockSpec((tile, double), lambda t: (t, 0))],
        out_specs=pl.BlockSpec((rows, double), lambda t: (0, 0)),
        out_shape=jax.ShapeDtypeStruct((rows, double), F32),
        compiler_params=params(),
        cost_estimate=cost(4 * rows * width * double, 4 * rows * width + 2 * double * width),
        name="direct_term",
    )(me, counts, data_real, data_imag, panel)


def swap(value, mask):
    return lax.ppermute(value, AXIS, [(i, i ^ mask) for i in range(lax.axis_size(AXIS))])


def picked(masks, i):
    mask = masks[0]
    for at in range(1, len(masks)):
        mask = jnp.where(i == at, masks[at], mask)
    return mask


def mirror_part_kernel(width, masks, first, me_ref, counts_ref, real_ref, imag_ref, *refs):
    other_ref, near_ref, far_ref, held_ref, sems = refs[-5:]
    panel_t_ref = refs[4] if first else refs[0]
    rows = real_ref.shape[0]
    tile = width // TILES
    me = me_ref[0]
    dy, i = pl.program_id(0), pl.program_id(1)
    some = len(masks)
    mine = me * rows // tile

    def copies(at, mask):
        columns = pl.ds(pl.multiple_of((me ^ mask) // 2 * (2 * rows), 2 * rows), 2 * rows)
        return [
            pltpu.make_async_copy(
                ref.at[:, columns], held_ref.at[at, pl.ds(part * rows, rows)], sems.at[at, part]
            )
            for part, ref in enumerate((real_ref, imag_ref))
        ]

    @pl.when((dy == 0) & (i == 0))
    def _():
        for at in range(2 * some):
            for copy in copies(at, masks[at % some] ^ (2 * (at // some))):
                copy.start()
        if first:
            store_panel(own_panel(width, mine, counts_ref, *refs[:3]), refs[3], panel_t_ref)

    panel_t = panel_t_ref[...]
    at = dy * some + i
    mask = picked(masks, i) ^ (2 * dy)
    for copy in copies(at, mask):
        copy.wait()

    def term(turn):
        block = me ^ mask ^ turn
        scale = weight(counts_ref, mine, block * rows // tile, (1, rows))
        columns = pl.ds(pl.multiple_of(block % 2 * rows, rows), rows)
        return dot(panel_t, held_ref[at, :, columns]) * scale

    other_ref[0] = term(1).astype(BF16)

    @pl.when(dy == 0)
    def _():
        near_ref[0] = term(0)

    @pl.when(dy == 1)
    def _():
        far_ref[0] = term(0)


def mirror_part(me, counts, data_real, data_imag, panel, masks, after):
    rows, width = data_real.shape
    first = len(panel) == 3
    double = panel[0].shape[0]
    some = len(masks)
    shape = (1, double, rows)
    whole = lambda *dims: pl.BlockSpec(dims, lambda dy, i, me: (0,) * len(dims))
    spec = pltpu.PrefetchScalarGridSpec(
        num_scalar_prefetch=1,
        grid=(2, some),
        in_specs=[whole_smem(), anywhere(), anywhere()]
        + [whole_vmem()] * len(panel)
        + [anywhere()] * len(after),
        out_specs=([whole(rows, double), whole(double, 2 * rows)] if first else [])
        + [
            pl.BlockSpec(shape, lambda dy, i, me: (dy * some + i, 0, 0)),
            pl.BlockSpec(shape, lambda dy, i, me: (jnp.where(dy == 0, i, some - 1), 0, 0)),
            pl.BlockSpec(shape, lambda dy, i, me: (jnp.where(dy == 0, 0, i), 0, 0)),
        ],
        scratch_shapes=[
            pltpu.VMEM((2 * some, 2 * rows, 2 * rows), BF16),
            pltpu.SemaphoreType.DMA((2 * some, 2)),
        ],
    )
    panel_shapes = [
        jax.ShapeDtypeStruct((rows, double), BF16),
        jax.ShapeDtypeStruct((double, 2 * rows), BF16),
    ]
    return pl.pallas_call(
        functools.partial(mirror_part_kernel, width, masks, first),
        grid_spec=spec,
        out_shape=(panel_shapes if first else [])
        + [
            jax.ShapeDtypeStruct((2 * some, double, rows), BF16),
            jax.ShapeDtypeStruct((some, double, rows), F32),
            jax.ShapeDtypeStruct((some, double, rows), F32),
        ],
        compiler_params=params(24),
        cost_estimate=cost(MIRROR_COST, 0),
        name="mirror_part",
    )(me, counts, data_real, data_imag, *panel, *after)


def ordered(value, after):
    return lax.optimization_barrier((value, after))[0]


def direct_part_kernel(
    width, masks, mirrors, me_ref, counts_ref, real_ref, imag_ref, panel_ref, *refs
):
    rows = real_ref.shape[0]
    tile = width // TILES
    k = pl.program_id(0)
    mine = me_ref[0] * rows // tile
    block = me_ref[0] ^ picked(masks, k)
    scale = weight(counts_ref, mine, block * rows // tile, (1, panel_ref.shape[2]))
    found = direct_block(real_ref[...], imag_ref[...], panel_ref[0]) * scale
    sum_refs, (total_ref, *out_refs) = (refs[:-3], refs[-1:] + refs[-3:-1]) if mirrors else (
        refs[:-1],
        refs[-1:],
    )

    @pl.when(k == 0)
    def _():
        total = found
        if mirrors:
            mirror = sum_refs[-1][...].astype(F32)
            for ref in sum_refs[1:-1]:
                mirror += ref[...].astype(F32)
            total += jnp.transpose(mirror)
        total_ref[...] = total + sum_refs[0][...] if sum_refs else total

    @pl.when(k > 0)
    def _():
        total_ref[...] += found

    if mirrors:
        factor = -1.0 / math.sqrt(width)
        count = panel_ref.shape[2] // 2

        @pl.when(k == len(masks) - 1)
        def _():
            out_refs[0][...] = factor * total_ref[:, :count]
            out_refs[1][...] = factor * total_ref[:, count:]


def direct_part(me, counts, data_real, data_imag, panels, before, masks, mirrors=()):
    rows, width = data_real.shape
    double = panels.shape[2]
    block = pl.BlockSpec((rows, rows), lambda k, me: (0, me[0] ^ picked(masks, k)))
    outs = [(rows, double // 2)] * 2 if mirrors else [(rows, double)]
    spec = pltpu.PrefetchScalarGridSpec(
        num_scalar_prefetch=1,
        grid=(len(masks),),
        in_specs=[whole_smem(), block, block, pl.BlockSpec((1, rows, double), lambda k, me: (k, 0, 0))]
        + [whole_vmem()] * (len(before) + len(mirrors)),
        out_specs=[pl.BlockSpec(shape, lambda k, me: (0, 0)) for shape in outs],
        scratch_shapes=[pltpu.VMEM((rows, double), F32)] if mirrors else [],
    )
    return pl.pallas_call(
        functools.partial(direct_part_kernel, width, masks, bool(mirrors)),
        grid_spec=spec,
        out_shape=[jax.ShapeDtypeStruct(shape, F32) for shape in outs],
        compiler_params=params(),
        cost_estimate=cost(DIRECT_COST, 0),
        name="direct_part",
    )(me, counts, data_real, data_imag, panels, *before, *mirrors)


def levels(me, counts, data_real, data_imag, rowpart, colpart, col):
    data = (in_hbm(data_real), in_hbm(data_imag))
    panel, panel_t, other, own, own_far = mirror_part(
        me, counts, *data, [rowpart, colpart, col], (HIGH, HIGH | LOW), []
    )
    high, low, beside = swap(panel, HIGH), swap(panel, LOW), swap(panel, Y)

    def to_y(other, own):
        got = swap(other, CORE)
        some = own.shape[0]
        return (own + got[some:].astype(F32)).astype(BF16), got[:some]

    def over_y(sent, own, got):
        return own + got.astype(F32) + swap(sent, Y).astype(F32)

    sent, got = to_y(other, own_far)
    other_here, own_here, own_here_far = mirror_part(me, counts, *data, [panel_t], (0, LOW), [sent])
    total = over_y(sent, own, got)
    to_low = total[1].astype(BF16)

    low, high, beside = ordered([low, high, beside], [sent, own_here])
    direct = []

    def add(panels, masks, mirrors=()):
        direct[:] = direct_part(me, counts, *data, panels, direct, masks, mirrors)

    add(ordered(panel[None], high), (0,))
    sent, got = to_y(ordered(other_here, high), ordered(own_here_far, high))
    total = total[0] + ordered(swap(to_low, LOW), [sent]).astype(F32)
    mirrors = [swap(total.astype(BF16), HIGH)]
    low_beside = ordered(swap(low, Y), [sent, total])
    both = ordered(swap(high, LOW), [sent, to_low])
    column = jnp.stack([panel, low, high, both])
    late = swap(ordered(jnp.stack([high, both]), [sent]), Y)
    early = jnp.stack([beside, low_beside])
    add(jnp.concatenate([column[1:], early]), (LOW, HIGH, HIGH | LOW, Y, Y | LOW))
    add(swap(column, CORE), (CORE, CORE | LOW, CORE | HIGH, CORE | HIGH | LOW))
    total = own_here + got.astype(F32) + swap(sent, Y).astype(F32)
    mirrors += [total[0], swap(total[1].astype(BF16), LOW)]
    add(swap(early, CORE), (Y | CORE, Y | CORE | LOW))
    late = ordered(late, direct + mirrors)
    add(late, (Y | HIGH, Y | HIGH | LOW))
    add(swap(late, CORE), (Y | CORE | HIGH, Y | CORE | HIGH | LOW), mirrors)
    return tuple(direct)


def finish_kernel(factor, direct_ref, mirror_ref, real_ref, imag_ref):
    count = real_ref.shape[1]
    total = factor * (direct_ref[...] + jnp.transpose(mirror_ref[...]))
    real_ref[...] = total[:, :count]
    imag_ref[...] = total[:, count:]


def finish(direct, mirror, width):
    rows, double = direct.shape
    shape = jax.ShapeDtypeStruct((rows, double // 2), F32)
    return pl.pallas_call(
        functools.partial(finish_kernel, -1.0 / math.sqrt(width)),
        in_specs=[whole_vmem()] * 2,
        out_specs=[whole_vmem()] * 2,
        out_shape=[shape, shape],
        compiler_params=params(),
        cost_estimate=cost(4 * rows * double, 10 * rows * double),
        name="finish",
    )(direct, mirror)


def shards(data_real, data_imag, counts, source_cols):
    rows, width = data_real.shape
    groups = width // rows
    count = source_cols.shape[0]
    cap = min(rows, count, -(-2 * count // groups // 8) * 8)
    col = source_cols.reshape(count, 1)
    row = source_cols.reshape(1, count)
    me = lax.axis_index(AXIS).reshape(1)

    def exchange(which):
        sent = own_source_rows(me, data_real, data_imag, source_cols, which, cap)
        return lax.all_to_all(sent, AXIS, split_axis=0, concat_axis=0)

    first = jnp.zeros((1,), jnp.int32)
    got = exchange(first)
    colpart = own_source_cols(data_real, data_imag, row, width // TILES)
    rowpart = select_rows(got, col, first, cap)

    owner = source_cols // rows
    most = jnp.max(jnp.sum(owner[:, None] == jnp.arange(groups)[None, :], axis=0, dtype=jnp.int32))

    def further(rowpart):
        def body(which, held):
            one = which.reshape(1)
            return held + select_rows(exchange(one), col, one, cap)

        return lax.fori_loop(1, (most + cap - 1) // cap, body, rowpart)

    rowpart = lax.cond(most > cap, further, lambda rowpart: rowpart, rowpart)
    if rows % 128 == 0 and groups == 16:
        return levels(me, counts, data_real, data_imag, rowpart, colpart, col)
    panel, panel_t = panel_only(me, counts, rowpart, colpart, col, width)
    full = lax.all_gather(panel, AXIS, axis=0, tiled=True)
    partial = mirror_term(me, counts, data_real, data_imag, panel_t)
    mirror = lax.psum_scatter(partial, AXIS, scatter_dimension=0, tiled=False)
    direct = direct_term(me, counts, data_real, data_imag, full)
    return tuple(finish(direct, mirror, width))


def solution(mesh):
    placed = (P(("freq", "row"), None), P(("freq", "row"), None), P(), P())
    return jax.shard_map(
        shards,
        mesh=mesh,
        in_specs=placed,
        out_specs=(P(("freq", "row"), None), P(("freq", "row"), None)),
        check_vma=False,
    )
```

profile of v0, /device:TPU:0, one launch (start us, length us, event | category | flops | bytes accessed | tf_op | source)
XLA Modules:
  0.0 91.7 jit_solution(8229083040050357786)
XLA Ops:
  0.6 0.0 copy-start.1
  0.6 5.3 %own_source_rows.2 = bf16[16,32,512]{2,1,0:T(8,128)(2,1)} custom-call(s32[1]{0:T(128)} %constant.47.clone.1.round_ref, s32[1]{0:T(128)} %bitcast.1.me_ref, s32[128]{0:T(128)} %col_ref.1, bf16[512,8192]{1,0:T(8,128)(2,1)} %real_ref.19, bf16[512,8192]{1,0:T(8,128)(2,1)} %imag_ref.19), custom_call_target="tpu_custom_call" | custom-call | bytes 262144 | tf_op jit(solution)/shard_map/own_source_rows/pallas_call | solution.py:109
  5.9 9.3 %all-to-all-start.1 = ((bf16[16,32,512]{2,1,0:T(8,128)(2,1)}), bf16[16,32,512]{2,1,0:T(8,128)(2,1)S(1)}, u32[]{:S(2)}, u32[]{:S(2)}) async-start(bf16[16,32,512]{2,1,0:T(8,128)(2,1)} %own_source_rows.2), calls=%async_computation.1 | async-start | bytes 1048576 | tf_op jit(solution)/shard_map/all_to_all | solution.py:562
  15.2 0.0 copy-done.1
  15.3 0.1 convert_reduce_fusion
  15.4 0.6 reduce_max.9
  16.7 0.1 copy.9.col_ref.refs_2_
  16.8 10.5 %own_source_cols.1.refs_1_ = bf16[256,512]{1,0:T(8,128)(2,1)S(1)} custom-call(bf16[512,8192]{1,0:T(8,128)(2,1)} %real_ref.19, bf16[512,8192]{1,0:T(8,128)(2,1)} %imag_ref.19, s32[1,128]{1,0:T(1,128)S(1)} %bitcast.37), custom_call_target="tpu_custom_call" | custom-call | flops 2147483648 | bytes 16777216 | tf_op jit(solution)/shard_map/own_source_cols/pallas_call | solution.py:149
  27.3 2.4 %all-to-all-done.1.got_ref = bf16[16,32,512]{2,1,0:T(8,128)(2,1)S(1)} async-done(((bf16[16,32,512]{2,1,0:T(8,128)(2,1)}), bf16[16,32,512]{2,1,0:T(8,128)(2,1)S(1)}, u32[]{:S(2)}, u32[]{:S(2)}) %all-to-all-start.1) | async-done | bytes 524320 | tf_op jit(solution)/shard_map/all_to_all | solution.py:562
  29.7 0.6 select_rows.2
  30.3 0.0 copy-start
  30.3 0.7 copy-done
  31.0 6.3 %mirror_part.2 = (bf16[512,256]{1,0:T(8,128)(2,1)S(1)}, bf16[256,1024]{1,0:T(8,128)(2,1)S(1)}, bf16[4,256,512]{2,1,0:T(8,128)(2,1)S(1)}, f32[2,256,512]{2,1,0:T(8,128)S(1)}, f32[2,256,512]{2,1,0:T(8,128)S(1)}) custom-call(s32[1]{0:T(128)} %bitcast.1.me_ref, s32[8,8]{1,0:T(8,128)S(1)} %copy-done, bf16[512,8192]{1,0:T(8,128)(2,1)} %real_ref.19, ...), custom_call_target="tpu_custom_call" | custom-call | flops 10000000000 | tf_op jit(solution)/shard_map/mirror_part/pallas_call | solution.py:403
  37.2 0.1 collective-permute-start.3
  37.3 1.2 %collective-permute-start.2 = (bf16[512,256]{1,0:T(8,128)(2,1)S(1)}, bf16[512,256]{1,0:T(8,128)(2,1)S(1)}, u32[]{:S(2)}, u32[]{:S(2)}) collective-permute-start(bf16[512,256]{1,0:T(8,128)(2,1)S(1)} %get-tuple-element.89), channel_id=1, source_target_pairs={{0,2},{1,3},{2,0},{3,1},{4,6},{5,7},{6,4},{7,5},{8,10},{9,11},{10,... | collective-permute-start | bytes 786440 | tf_op jit(solution)/shard_map/ppermute | solution.py:315
  38.5 1.2 %collective-permute-start.1 = (bf16[512,256]{1,0:T(8,128)(2,1)S(1)}, bf16[512,256]{1,0:T(8,128)(2,1)S(1)}, u32[]{:S(2)}, u32[]{:S(2)}) collective-permute-start(bf16[512,256]{1,0:T(8,128)(2,1)S(1)} %get-tuple-element.89), channel_id=1, source_target_pairs={{0,8},{1,9},{2,10},{3,11},{4,12},{5,13},{6,14},{7,15},{8,0},{9,1},... | collective-permute-start | bytes 786440 | tf_op jit(solution)/shard_map/ppermute | solution.py:315
  39.7 1.7 %collective-permute-start = (bf16[512,256]{1,0:T(8,128)(2,1)S(1)}, bf16[512,256]{1,0:T(8,128)(2,1)S(1)}, u32[]{:S(2)}, u32[]{:S(2)}) collective-permute-start(bf16[512,256]{1,0:T(8,128)(2,1)S(1)} %get-tuple-element.89), channel_id=1, source_target_pairs={{0,4},{1,5},{2,6},{3,7},{4,0},{5,1},{6,2},{7,3},{8,12},{9,13},{10,... | collective-permute-start | bytes 786440 | tf_op jit(solution)/shard_map/ppermute | solution.py:315
  41.4 0.0 collective-permute-done.3
  41.5 0.2 add_convert_fusion.1.refs_1_
  41.6 0.5 collective-permute-start.6
  42.1 6.1 %mirror_part.3 = (bf16[4,256,512]{2,1,0:T(8,128)(2,1)S(1)}, f32[2,256,512]{2,1,0:T(8,128)S(1)}, f32[2,256,512]{2,1,0:T(8,128)S(1)}) custom-call(s32[1]{0:T(128)} %bitcast.1.me_ref, s32[8,8]{1,0:T(8,128)S(1)} %copy-done, bf16[512,8192]{1,0:T(8,128)(2,1)} %real_ref.19, bf16[512,8192]{1,0:T(8,128)(2,1)} %imag_ref.19, ...), custom_call_target="tpu_custom_call" | custom-call | flops 10000000000 | tf_op jit(solution)/shard_map/mirror_part/pallas_call | solution.py:403
  48.2 0.0 collective-permute-done.2
  48.2 4.8 %collective-permute-done.1 = bf16[512,256]{1,0:T(8,128)(2,1)S(1)} collective-permute-done((bf16[512,256]{1,0:T(8,128)(2,1)S(1)}, bf16[512,256]{1,0:T(8,128)(2,1)S(1)}, u32[]{:S(2)}, u32[]{:S(2)}) %collective-permute-start.1) | collective-permute-done | bytes 262176 | tf_op jit(solution)/shard_map/ppermute | solution.py:315
  53.0 0.0 collective-permute-done
  53.0 0.9 %collective-permute-start.4 = (bf16[512,256]{1,0:T(8,128)(2,1)S(1)}, bf16[512,256]{1,0:T(8,128)(2,1)S(1)}, u32[]{:S(2)}, u32[]{:S(2)}) collective-permute-start(bf16[512,256]{1,0:T(8,128)(2,1)S(1)} %collective-permute-done.1), channel_id=1, source_target_pairs={{0,4},{1,5},{2,6},{3,7},{4,0},{5,1},{6,2},{7,3},{8,12},{9,13},{10,... | collective-permute-start | bytes 786440 | tf_op jit(solution)/shard_map/ppermute | solution.py:315
  54.0 1.8 %collective-permute-start.8 = (bf16[512,256]{1,0:T(8,128)(2,1)S(1)}, bf16[512,256]{1,0:T(8,128)(2,1)S(1)}, u32[]{:S(2)}, u32[]{:S(2)}) collective-permute-start(bf16[512,256]{1,0:T(8,128)(2,1)S(1)} %collective-permute-done), channel_id=1, source_target_pairs={{0,2},{1,3},{2,0},{3,1},{4,6},{5,7},{6,4},{7,5},{8,10},{9,11},{10,... | collective-permute-start | bytes 786440 | tf_op jit(solution)/shard_map/ppermute | solution.py:315
  55.7 0.0 collective-permute-start.5
  55.7 1.7 %direct_part.6.refs_0_ = f32[512,256]{1,0:T(8,128)S(1)} custom-call(s32[1]{0:T(128)} %bitcast.1.me_ref, s32[8,8]{1,0:T(8,128)S(1)} %copy-done, bf16[512,8192]{1,0:T(8,128)(2,1)} %real_ref.19, bf16[512,8192]{1,0:T(8,128)(2,1)} %imag_ref.19, bf16[1,512,256]{2,1,0:T(8,128)(2,1)S(1)} %bitcast.27), custom_call_target="tpu_custom_call" | custom-call | flops 2000000000 | tf_op jit(solution)/shard_map/direct_part/pallas_call | solution.py:474
  57.4 0.3 collective-permute-done.6
  57.7 0.2 convert_add_fusion.1
  58.0 1.8 %collective-permute-start.9 = (bf16[256,512]{1,0:T(8,128)(2,1)S(1)}, bf16[256,512]{1,0:T(8,128)(2,1)S(1)}, u32[]{:S(2)}, u32[]{:S(2)}) collective-permute-start(bf16[256,512]{1,0:T(8,128)(2,1)S(1)} %fusion.1), channel_id=1, source_target_pairs={{0,4},{1,5},{2,6},{3,7},{4,0},{5,1},{6,2},{7,3},{8,12},{9,13},{10,... | collective-permute-start | bytes 786440 | tf_op jit(solution)/shard_map/ppermute | solution.py:315
  59.8 0.0 collective-permute-done.5
  59.8 0.2 add_convert_fusion
  60.0 1.0 %collective-permute-start.13 = (bf16[2,256,512]{2,1,0:T(8,128)(2,1)S(1)}, bf16[2,256,512]{2,1,0:T(8,128)(2,1)S(1)}, u32[]{:S(2)}, u32[]{:S(2)}) collective-permute-start(bf16[2,256,512]{2,1,0:T(8,128)(2,1)S(1)} %add_convert_fusion), channel_id=1, source_target_pairs={{0,2},{1,3},{2,0},{3,1},{4,6},{5,7},{6,4},{7,5},{8,10},{9,11},{10,... | collective-permute-start | bytes 1572872 | tf_op jit(solution)/shard_map/ppermute | solution.py:315
  60.9 5.6 %collective-permute-done.9 = bf16[256,512]{1,0:T(8,128)(2,1)S(1)} collective-permute-done((bf16[256,512]{1,0:T(8,128)(2,1)S(1)}, bf16[256,512]{1,0:T(8,128)(2,1)S(1)}, u32[]{:S(2)}, u32[]{:S(2)}) %collective-permute-start.9) | collective-permute-done | bytes 262176 | tf_op jit(solution)/shard_map/ppermute | solution.py:315
  66.5 0.1 fusion
  66.6 1.6 %collective-permute-start.12 = (bf16[256,512]{1,0:T(8,128)(2,1)S(1)}, bf16[256,512]{1,0:T(8,128)(2,1)S(1)}, u32[]{:S(2)}, u32[]{:S(2)}) collective-permute-start(bf16[256,512]{1,0:T(8,128)(2,1)S(1)} %fusion), channel_id=1, source_target_pairs={{0,8},{1,9},{2,10},{3,11},{4,12},{5,13},{6,14},{7,15},{8,0},{9,1},... | collective-permute-start | bytes 786440 | tf_op jit(solution)/shard_map/ppermute | solution.py:315
  68.2 0.0 collective-permute-done.8
  68.2 0.0 collective-permute-done.4
  68.2 0.1 pad_maximum_fusion.1
  68.3 0.1 pad_maximum_fusion.2
  68.3 0.1 collective-permute-start.10
  68.4 0.9 %collective-permute-start.7 = (bf16[2,512,256]{2,1,0:T(8,128)(2,1)S(1)}, bf16[2,512,256]{2,1,0:T(8,128)(2,1)S(1)}, u32[]{:S(2)}, u32[]{:S(2)}) collective-permute-start(bf16[2,512,256]{2,1,0:T(8,128)(2,1)S(1)} %pad_maximum_fusion.1), channel_id=1, source_target_pairs={{0,2},{1,3},{2,0},{3,1},{4,6},{5,7},{6,4},{7,5},{8,10},{9,11},{10,... | collective-permute-start | bytes 1572872 | tf_op jit(solution)/shard_map/ppermute | solution.py:315
  69.3 0.1 pad_maximum_fusion
  69.5 0.2 collective-permute-start.11
  69.8 5.3 %direct_part.7.refs_0_ = f32[512,256]{1,0:T(8,128)S(1)} custom-call(s32[1]{0:T(128)} %bitcast.1.me_ref, s32[8,8]{1,0:T(8,128)S(1)} %copy-done, bf16[512,8192]{1,0:T(8,128)(2,1)} %real_ref.19, bf16[512,8192]{1,0:T(8,128)(2,1)} %imag_ref.19, bf16[5,512,256]{2,1,0:T(8,128)(2,1)S(1)} %constant_dynamic-update-slice_fusion.panel_ref, ...), custom_call_target="tpu_custom_call" | custom-call | flops 2000000000 | tf_op jit(solution)/shard_map/direct_part/pallas_call | solution.py:474
  75.1 0.0 collective-permute-done.13
  75.1 0.2 convert_add_fusion
  75.3 1.3 %collective-permute-start.14 = (bf16[256,512]{1,0:T(8,128)(2,1)S(1)}, bf16[256,512]{1,0:T(8,128)(2,1)S(1)}, u32[]{:S(2)}, u32[]{:S(2)}) collective-permute-start(bf16[256,512]{1,0:T(8,128)(2,1)S(1)} %fusion.2), channel_id=1, source_target_pairs={{0,4},{1,5},{2,6},{3,7},{4,0},{5,1},{6,2},{7,3},{8,12},{9,13},{10,... | collective-permute-start | bytes 786440 | tf_op jit(solution)/shard_map/ppermute | solution.py:315
  76.7 0.0 collective-permute-done.11.panel_ref
  76.7 4.1 %direct_part.8.refs_0_ = f32[512,256]{1,0:T(8,128)S(1)} custom-call(s32[1]{0:T(128)} %bitcast.1.me_ref, s32[8,8]{1,0:T(8,128)S(1)} %copy-done, bf16[512,8192]{1,0:T(8,128)(2,1)} %real_ref.19, bf16[512,8192]{1,0:T(8,128)(2,1)} %imag_ref.19, bf16[4,512,256]{2,1,0:T(8,128)(2,1)S(1)} %collective-permute-done.11.panel_ref, f32[512,256]{1,0:T(8,128)S(1)} %direct_part.7.refs_0_), custom_call_target="tpu_custom_call" | custom-call | flops 2000000000 | tf_op jit(solution)/shard_map/direct_part/pallas_call | solution.py:474
  80.8 0.0 collective-permute-done.10.panel_ref
  80.8 2.3 %direct_part.9.refs_0_ = f32[512,256]{1,0:T(8,128)S(1)} custom-call(s32[1]{0:T(128)} %bitcast.1.me_ref, s32[8,8]{1,0:T(8,128)S(1)} %copy-done, bf16[512,8192]{1,0:T(8,128)(2,1)} %real_ref.19, bf16[512,8192]{1,0:T(8,128)(2,1)} %imag_ref.19, bf16[2,512,256]{2,1,0:T(8,128)(2,1)S(1)} %collective-permute-done.10.panel_ref, f32[512,256]{1,0:T(8,128)S(1)} %direct_part.8.refs_0_), custom_call_target="tpu_custom_call" | custom-call | flops 2000000000 | tf_op jit(solution)/shard_map/direct_part/pallas_call | solution.py:474
  83.2 0.0 collective-permute-done.12.refs_1_
  83.2 2.2 %collective-permute-done.7.panel_ref = bf16[2,512,256]{2,1,0:T(8,128)(2,1)S(1)} collective-permute-done((bf16[2,512,256]{2,1,0:T(8,128)(2,1)S(1)}, bf16[2,512,256]{2,1,0:T(8,128)(2,1)S(1)}, u32[]{:S(2)}, u32[]{:S(2)}) %collective-permute-start.7) | collective-permute-done | bytes 524320 | tf_op jit(solution)/shard_map/ppermute | solution.py:315
  85.4 0.7 collective-permute-done.14.refs_3_
  86.1 0.1 collective-permute-start.15
  86.1 2.3 %direct_part.10.refs_0_ = f32[512,256]{1,0:T(8,128)S(1)} custom-call(s32[1]{0:T(128)} %bitcast.1.me_ref, s32[8,8]{1,0:T(8,128)S(1)} %copy-done, bf16[512,8192]{1,0:T(8,128)(2,1)} %real_ref.19, bf16[512,8192]{1,0:T(8,128)(2,1)} %imag_ref.19, bf16[2,512,256]{2,1,0:T(8,128)(2,1)S(1)} %collective-permute-done.7.panel_ref, f32[512,256]{1,0:T(8,128)S(1)} %direct_part.9.refs_0_), custom_call_target="tpu_custom_call" | custom-call | flops 2000000000 | tf_op jit(solution)/shard_map/direct_part/pallas_call | solution.py:474
  88.4 0.0 collective-permute-done.15.panel_ref
  88.4 3.3 %direct_part.11 = (f32[512,128]{1,0:T(8,128)}, f32[512,128]{1,0:T(8,128)}) custom-call(s32[1]{0:T(128)} %bitcast.1.me_ref, s32[8,8]{1,0:T(8,128)S(1)} %copy-done, bf16[512,8192]{1,0:T(8,128)(2,1)} %real_ref.19, bf16[512,8192]{1,0:T(8,128)(2,1)} %imag_ref.19, bf16[2,512,256]{2,1,0:T(8,128)(2,1)S(1)} %collective-permute-done.15.panel_ref, ...), custom_call_target="tpu_custom_call" | custom-call | flops 2000000000 | tf_op jit(solution)/shard_map/direct_part/pallas_call | solution.py:474
  (10 shorter events, 0.2 us)
Async XLA Ops:
  0.6 14.6 %copy-start.1 = (s32[128]{0:T(128)S(1)}, s32[128]{0:T(128)}, u32[]{:S(2)}) copy-start(s32[128]{0:T(128)} %col_ref.1) | copy-start | bytes 1540
  5.9 23.7 %all-to-all-start.1 = ((bf16[16,32,512]{2,1,0:T(8,128)(2,1)}), bf16[16,32,512]{2,1,0:T(8,128)(2,1)S(1)}, u32[]{:S(2)}, u32[]{:S(2)}) async-start(bf16[16,32,512]{2,1,0:T(8,128)(2,1)} %own_source_rows.2), calls=%async_computation.1 | async-start | bytes 1048576 | tf_op jit(solution)/shard_map/all_to_all | solution.py:562
  30.3 0.7 copy-start
  37.2 4.2 %collective-permute-start.3 = (bf16[4,256,512]{2,1,0:T(8,128)(2,1)S(1)}, bf16[4,256,512]{2,1,0:T(8,128)(2,1)S(1)}, u32[]{:S(2)}, u32[]{:S(2)}) collective-permute-start(bf16[4,256,512]{2,1,0:T(8,128)(2,1)S(1)} %get-tuple-element.91), channel_id=1, source_target_pairs={{0,1},{1,0},{2,3},{3,2},{4,5},{5,4},{6,7},{7,6},{8,9},{9,8},{10,11... | collective-permute-start | bytes 3145736 | tf_op jit(solution)/shard_map/ppermute | solution.py:315
  37.3 10.9 %collective-permute-start.2 = (bf16[512,256]{1,0:T(8,128)(2,1)S(1)}, bf16[512,256]{1,0:T(8,128)(2,1)S(1)}, u32[]{:S(2)}, u32[]{:S(2)}) collective-permute-start(bf16[512,256]{1,0:T(8,128)(2,1)S(1)} %get-tuple-element.89), channel_id=1, source_target_pairs={{0,2},{1,3},{2,0},{3,1},{4,6},{5,7},{6,4},{7,5},{8,10},{9,11},{10,... | collective-permute-start | bytes 786440 | tf_op jit(solution)/shard_map/ppermute | solution.py:315
  38.5 14.5 %collective-permute-start.1 = (bf16[512,256]{1,0:T(8,128)(2,1)S(1)}, bf16[512,256]{1,0:T(8,128)(2,1)S(1)}, u32[]{:S(2)}, u32[]{:S(2)}) collective-permute-start(bf16[512,256]{1,0:T(8,128)(2,1)S(1)} %get-tuple-element.89), channel_id=1, source_target_pairs={{0,8},{1,9},{2,10},{3,11},{4,12},{5,13},{6,14},{7,15},{8,0},{9,1},... | collective-permute-start | bytes 786440 | tf_op jit(solution)/shard_map/ppermute | solution.py:315
  39.7 13.3 %collective-permute-start = (bf16[512,256]{1,0:T(8,128)(2,1)S(1)}, bf16[512,256]{1,0:T(8,128)(2,1)S(1)}, u32[]{:S(2)}, u32[]{:S(2)}) collective-permute-start(bf16[512,256]{1,0:T(8,128)(2,1)S(1)} %get-tuple-element.89), channel_id=1, source_target_pairs={{0,4},{1,5},{2,6},{3,7},{4,0},{5,1},{6,2},{7,3},{8,12},{9,13},{10,... | collective-permute-start | bytes 786440 | tf_op jit(solution)/shard_map/ppermute | solution.py:315
  41.6 16.1 %collective-permute-start.6 = (bf16[2,256,512]{2,1,0:T(8,128)(2,1)S(1)}, bf16[2,256,512]{2,1,0:T(8,128)(2,1)S(1)}, u32[]{:S(2)}, u32[]{:S(2)}) collective-permute-start(bf16[2,256,512]{2,1,0:T(8,128)(2,1)S(1)} %add_convert_fusion.1.refs_1_), channel_id=1, source_target_pairs={{0,2},{1,3},{2,0},{3,1},{4,6},{5,7},{6,4},{7,5},{8,10},{9,11},{10,... | collective-permute-start | bytes 1572872 | tf_op jit(solution)/shard_map/ppermute | solution.py:315
  53.0 15.2 %collective-permute-start.4 = (bf16[512,256]{1,0:T(8,128)(2,1)S(1)}, bf16[512,256]{1,0:T(8,128)(2,1)S(1)}, u32[]{:S(2)}, u32[]{:S(2)}) collective-permute-start(bf16[512,256]{1,0:T(8,128)(2,1)S(1)} %collective-permute-done.1), channel_id=1, source_target_pairs={{0,4},{1,5},{2,6},{3,7},{4,0},{5,1},{6,2},{7,3},{8,12},{9,13},{10,... | collective-permute-start | bytes 786440 | tf_op jit(solution)/shard_map/ppermute | solution.py:315
  54.0 14.2 %collective-permute-start.8 = (bf16[512,256]{1,0:T(8,128)(2,1)S(1)}, bf16[512,256]{1,0:T(8,128)(2,1)S(1)}, u32[]{:S(2)}, u32[]{:S(2)}) collective-permute-start(bf16[512,256]{1,0:T(8,128)(2,1)S(1)} %collective-permute-done), channel_id=1, source_target_pairs={{0,2},{1,3},{2,0},{3,1},{4,6},{5,7},{6,4},{7,5},{8,10},{9,11},{10,... | collective-permute-start | bytes 786440 | tf_op jit(solution)/shard_map/ppermute | solution.py:315
  55.7 4.1 %collective-permute-start.5 = (bf16[4,256,512]{2,1,0:T(8,128)(2,1)S(1)}, bf16[4,256,512]{2,1,0:T(8,128)(2,1)S(1)}, u32[]{:S(2)}, u32[]{:S(2)}) collective-permute-start(bf16[4,256,512]{2,1,0:T(8,128)(2,1)S(1)} %get-tuple-element.98), channel_id=1, source_target_pairs={{0,1},{1,0},{2,3},{3,2},{4,5},{5,4},{6,7},{7,6},{8,9},{9,8},{10,11... | collective-permute-start | bytes 3145736 | tf_op jit(solution)/shard_map/ppermute | solution.py:315
  58.0 8.5 %collective-permute-start.9 = (bf16[256,512]{1,0:T(8,128)(2,1)S(1)}, bf16[256,512]{1,0:T(8,128)(2,1)S(1)}, u32[]{:S(2)}, u32[]{:S(2)}) collective-permute-start(bf16[256,512]{1,0:T(8,128)(2,1)S(1)} %fusion.1), channel_id=1, source_target_pairs={{0,4},{1,5},{2,6},{3,7},{4,0},{5,1},{6,2},{7,3},{8,12},{9,13},{10,... | collective-permute-start | bytes 786440 | tf_op jit(solution)/shard_map/ppermute | solution.py:315
  60.0 15.1 %collective-permute-start.13 = (bf16[2,256,512]{2,1,0:T(8,128)(2,1)S(1)}, bf16[2,256,512]{2,1,0:T(8,128)(2,1)S(1)}, u32[]{:S(2)}, u32[]{:S(2)}) collective-permute-start(bf16[2,256,512]{2,1,0:T(8,128)(2,1)S(1)} %add_convert_fusion), channel_id=1, source_target_pairs={{0,2},{1,3},{2,0},{3,1},{4,6},{5,7},{6,4},{7,5},{8,10},{9,11},{10,... | collective-permute-start | bytes 1572872 | tf_op jit(solution)/shard_map/ppermute | solution.py:315
  66.6 16.6 %collective-permute-start.12 = (bf16[256,512]{1,0:T(8,128)(2,1)S(1)}, bf16[256,512]{1,0:T(8,128)(2,1)S(1)}, u32[]{:S(2)}, u32[]{:S(2)}) collective-permute-start(bf16[256,512]{1,0:T(8,128)(2,1)S(1)} %fusion), channel_id=1, source_target_pairs={{0,8},{1,9},{2,10},{3,11},{4,12},{5,13},{6,14},{7,15},{8,0},{9,1},... | collective-permute-start | bytes 786440 | tf_op jit(solution)/shard_map/ppermute | solution.py:315
  68.3 12.5 %collective-permute-start.10 = (bf16[2,512,256]{2,1,0:T(8,128)(2,1)S(1)}, bf16[2,512,256]{2,1,0:T(8,128)(2,1)S(1)}, u32[]{:S(2)}, u32[]{:S(2)}) collective-permute-start(bf16[2,512,256]{2,1,0:T(8,128)(2,1)S(1)} %pad_maximum_fusion.2), channel_id=1, source_target_pairs={{0,1},{1,0},{2,3},{3,2},{4,5},{5,4},{6,7},{7,6},{8,9},{9,8},{10,11... | collective-permute-start | bytes 1572872 | tf_op jit(solution)/shard_map/ppermute | solution.py:315
  68.4 17.0 %collective-permute-start.7 = (bf16[2,512,256]{2,1,0:T(8,128)(2,1)S(1)}, bf16[2,512,256]{2,1,0:T(8,128)(2,1)S(1)}, u32[]{:S(2)}, u32[]{:S(2)}) collective-permute-start(bf16[2,512,256]{2,1,0:T(8,128)(2,1)S(1)} %pad_maximum_fusion.1), channel_id=1, source_target_pairs={{0,2},{1,3},{2,0},{3,1},{4,6},{5,7},{6,4},{7,5},{8,10},{9,11},{10,... | collective-permute-start | bytes 1572872 | tf_op jit(solution)/shard_map/ppermute | solution.py:315
  69.5 7.2 %collective-permute-start.11 = (bf16[4,512,256]{2,1,0:T(8,128)(2,1)S(1)}, bf16[4,512,256]{2,1,0:T(8,128)(2,1)S(1)}, u32[]{:S(2)}, u32[]{:S(2)}) collective-permute-start(bf16[4,512,256]{2,1,0:T(8,128)(2,1)S(1)} %pad_maximum_fusion), channel_id=1, source_target_pairs={{0,1},{1,0},{2,3},{3,2},{4,5},{5,4},{6,7},{7,6},{8,9},{9,8},{10,11... | collective-permute-start | bytes 3145736 | tf_op jit(solution)/shard_map/ppermute | solution.py:315
  75.3 10.7 %collective-permute-start.14 = (bf16[256,512]{1,0:T(8,128)(2,1)S(1)}, bf16[256,512]{1,0:T(8,128)(2,1)S(1)}, u32[]{:S(2)}, u32[]{:S(2)}) collective-permute-start(bf16[256,512]{1,0:T(8,128)(2,1)S(1)} %fusion.2), channel_id=1, source_target_pairs={{0,4},{1,5},{2,6},{3,7},{4,0},{5,1},{6,2},{7,3},{8,12},{9,13},{10,... | collective-permute-start | bytes 786440 | tf_op jit(solution)/shard_map/ppermute | solution.py:315
  86.1 2.4 %collective-permute-start.15 = (bf16[2,512,256]{2,1,0:T(8,128)(2,1)S(1)}, bf16[2,512,256]{2,1,0:T(8,128)(2,1)S(1)}, u32[]{:S(2)}, u32[]{:S(2)}) collective-permute-start(bf16[2,512,256]{2,1,0:T(8,128)(2,1)S(1)} %collective-permute-done.7.panel_ref), channel_id=1, source_target_pairs={{0,1},{1,0},{2,3},{3,2},{4,5},{5,4},{6,7},{7,6},{8,9},{9,8},{10,11... | collective-permute-start | bytes 1572872 | tf_op jit(solution)/shard_map/ppermute | solution.py:315
where the time goes:
time: 92.1 us; the launch traced here: 91.7 us
  Pallas kernels  47.7 us (52%)
  starting transfers between devices  23.6 us (26%)
  waiting for transfers between devices  16 us (17%)
  other arithmetic  1.83 us (2%)
  between operations  1.58 us (2%)
  local copies, waits for them, and re-layouts  0.98 us (1%)
    pallas_call x6, Pallas kernels, direct_part(): pl.pallas_call(functools.partial(direct_part_kernel, width, masks, bool(m...  19 us
    ppermute x16, starting transfers between devices, swap(): lax.ppermute(value, AXIS, [(i, i ^ mask) for i in range(lax.axis_size(AXI...  14.3 us
    ppermute x16, waiting for transfers between devices, swap(): lax.ppermute(value, AXIS, [(i, i ^ mask) for i in range(lax.axis_size(AXI...  13.6 us
    pallas_call x2, Pallas kernels, mirror_part(): pl.pallas_call(functools.partial(mirror_part_kernel, width, masks, first)...  12.3 us
    pallas_call x1, Pallas kernels, own_source_cols(): pl.pallas_call(cols_kernel, grid=(width // step,), in_specs=[block, block...  10.5 us
    all_to_all x1, starting transfers between devices, exchange(): return lax.all_to_all(sent, AXIS, split_axis=0, concat_axis=0)  9.27 us
    pallas_call x1, Pallas kernels, own_source_rows(): pl.pallas_call(functools.partial(rows_kernel, cap), in_specs=[whole_smem(...  5.3 us
    all_to_all x1, waiting for transfers between devices, exchange(): return lax.all_to_all(sent, AXIS, split_axis=0, concat_axis=0)  2.43 us
  transfers between devices with their start and end apart: 17, of which 6 were waited for; matrix products, arithmetic and copies ran while one was open for 2% of the time, Pallas kernels for 35%

commit v1 on v0

--- a/solution.py
+++ b/solution.py
@@ -323,13 +323,12 @@
 
 
 def mirror_part_kernel(width, masks, first, me_ref, counts_ref, real_ref, imag_ref, *refs):
-    other_ref, near_ref, far_ref, held_ref, sems = refs[-5:]
+    other_ref, own_ref, held_ref, sems = refs[-4:]
     panel_t_ref = refs[4] if first else refs[0]
     rows = real_ref.shape[0]
     tile = width // TILES
     me = me_ref[0]
-    dy, i = pl.program_id(0), pl.program_id(1)
-    some = len(masks)
+    i = pl.program_id(0)
     mine = me * rows // tile
 
     def copies(at, mask):
@@ -341,59 +340,50 @@
             for part, ref in enumerate((real_ref, imag_ref))
         ]
 
-    @pl.when((dy == 0) & (i == 0))
+    @pl.when(i == 0)
     def _():
-        for at in range(2 * some):
-            for copy in copies(at, masks[at % some] ^ (2 * (at // some))):
+        for at, mask in enumerate(masks):
+            for copy in copies(at, mask):
                 copy.start()
         if first:
             store_panel(own_panel(width, mine, counts_ref, *refs[:3]), refs[3], panel_t_ref)
 
     panel_t = panel_t_ref[...]
-    at = dy * some + i
-    mask = picked(masks, i) ^ (2 * dy)
-    for copy in copies(at, mask):
+    mask = picked(masks, i)
+    for copy in copies(i, mask):
         copy.wait()
 
     def term(turn):
         block = me ^ mask ^ turn
         scale = weight(counts_ref, mine, block * rows // tile, (1, rows))
         columns = pl.ds(pl.multiple_of(block % 2 * rows, rows), rows)
-        return dot(panel_t, held_ref[at, :, columns]) * scale
+        return dot(panel_t, held_ref[i, :, columns]) * scale
 
     other_ref[0] = term(1).astype(BF16)
-
-    @pl.when(dy == 0)
-    def _():
-        near_ref[0] = term(0)
-
-    @pl.when(dy == 1)
-    def _():
-        far_ref[0] = term(0)
+    own_ref[0] = term(0)
 
 
 def mirror_part(me, counts, data_real, data_imag, panel, masks, after):
     rows, width = data_real.shape
     first = len(panel) == 3
     double = panel[0].shape[0]
-    some = len(masks)
+    blocks = len(masks)
     shape = (1, double, rows)
-    whole = lambda *dims: pl.BlockSpec(dims, lambda dy, i, me: (0,) * len(dims))
+    whole = lambda *dims: pl.BlockSpec(dims, lambda i, me: (0,) * len(dims))
     spec = pltpu.PrefetchScalarGridSpec(
         num_scalar_prefetch=1,
-        grid=(2, some),
+        grid=(blocks,),
         in_specs=[whole_smem(), anywhere(), anywhere()]
         + [whole_vmem()] * len(panel)
         + [anywhere()] * len(after),
         out_specs=([whole(rows, double), whole(double, 2 * rows)] if first else [])
         + [
-            pl.BlockSpec(shape, lambda dy, i, me: (dy * some + i, 0, 0)),
-            pl.BlockSpec(shape, lambda dy, i, me: (jnp.where(dy == 0, i, some - 1), 0, 0)),
-            pl.BlockSpec(shape, lambda dy, i, me: (jnp.where(dy == 0, 0, i), 0, 0)),
+            pl.BlockSpec(shape, lambda i, me: (i, 0, 0)),
+            pl.BlockSpec(shape, lambda i, me: (i, 0, 0)),
         ],
         scratch_shapes=[
-            pltpu.VMEM((2 * some, 2 * rows, 2 * rows), BF16),
-            pltpu.SemaphoreType.DMA((2 * some, 2)),
+            pltpu.VMEM((blocks, 2 * rows, 2 * rows), BF16),
+            pltpu.SemaphoreType.DMA((blocks, 2)),
         ],
     )
     panel_shapes = [
@@ -405,11 +395,10 @@
         grid_spec=spec,
         out_shape=(panel_shapes if first else [])
         + [
-            jax.ShapeDtypeStruct((2 * some, double, rows), BF16),
-            jax.ShapeDtypeStruct((some, double, rows), F32),
-            jax.ShapeDtypeStruct((some, double, rows), F32),
+            jax.ShapeDtypeStruct((blocks, double, rows), BF16),
+            jax.ShapeDtypeStruct((blocks, double, rows), F32),
         ],
-        compiler_params=params(24),
+        compiler_params=params(32),
         cost_estimate=cost(MIRROR_COST, 0),
         name="mirror_part",
     )(me, counts, data_real, data_imag, *panel, *after)
@@ -483,34 +472,33 @@
 
 def levels(me, counts, data_real, data_imag, rowpart, colpart, col):
     data = (in_hbm(data_real), in_hbm(data_imag))
-    panel, panel_t, other, own, own_far = mirror_part(
-        me, counts, *data, [rowpart, colpart, col], (HIGH, HIGH | LOW), []
+    panel, panel_t, other, own = mirror_part(
+        me, counts, *data, [rowpart, colpart, col], (Y | HIGH, Y | HIGH | LOW), []
     )
     high, low, beside = swap(panel, HIGH), swap(panel, LOW), swap(panel, Y)
-
-    def to_y(other, own):
-        got = swap(other, CORE)
-        some = own.shape[0]
-        return (own + got[some:].astype(F32)).astype(BF16), got[:some]
-
-    def over_y(sent, own, got):
-        return own + got.astype(F32) + swap(sent, Y).astype(F32)
-
-    sent, got = to_y(other, own_far)
-    other_here, own_here, own_here_far = mirror_part(me, counts, *data, [panel_t], (0, LOW), [sent])
-    total = over_y(sent, own, got)
-    to_low = total[1].astype(BF16)
-
-    low, high, beside = ordered([low, high, beside], [sent, own_here])
+    far_sent = (own + swap(other, CORE).astype(F32)).astype(BF16)
+    def part(masks, after):
+        return mirror_part(me, counts, *data, [panel_t], masks, after)
+
+    far_other, far_own = part((HIGH, HIGH | LOW), [far_sent])
+    other, own = part((0, LOW, Y, Y | LOW), [far_own])
+    arrived = swap(far_sent, Y).astype(F32)
+
+    low, high, beside = ordered([low, high, beside], [far_sent, own])
     direct = []
 
     def add(panels, masks, mirrors=()):
         direct[:] = direct_part(me, counts, *data, panels, direct, masks, mirrors)
 
     add(ordered(panel[None], high), (0,))
-    sent, got = to_y(ordered(other_here, high), ordered(own_here_far, high))
+    own = ordered(own, high)
+    got = swap(ordered(other, high), CORE)
+    sent = (own[2:] + got[2:].astype(F32)).astype(BF16)
+    total = far_own + swap(far_other, CORE).astype(F32) + arrived
+    to_low = total[1].astype(BF16)
     total = total[0] + ordered(swap(to_low, LOW), [sent]).astype(F32)
     mirrors = [swap(total.astype(BF16), HIGH)]
+
     low_beside = ordered(swap(low, Y), [sent, total])
     both = ordered(swap(high, LOW), [sent, to_low])
     column = jnp.stack([panel, low, high, both])
@@ -518,7 +506,7 @@
     early = jnp.stack([beside, low_beside])
     add(jnp.concatenate([column[1:], early]), (LOW, HIGH, HIGH | LOW, Y, Y | LOW))
     add(swap(column, CORE), (CORE, CORE | LOW, CORE | HIGH, CORE | HIGH | LOW))
-    total = own_here + got.astype(F32) + swap(sent, Y).astype(F32)
+    total = own[:2] + got[:2].astype(F32) + swap(sent, Y).astype(F32)
     mirrors += [total[0], swap(total[1].astype(BF16), LOW)]
     add(swap(early, CORE), (Y | CORE, Y | CORE | LOW))
     late = ordered(late, direct + mirrors)

time: 92.1 us -> 88.7 us (0.963)
  waiting for transfers between devices: 16 us -> 13 us
  starting transfers between devices: 23.6 us -> 21.3 us
  Pallas kernels: 47.7 us -> 49.1 us
    ppermute x16 -> x17, waiting for transfers between devices: 13.6 us -> 10.5 us  [swap(): lax.ppermute(value, AXIS, [(i, i ^ mask) for i in range(lax.axis_size(AXI...]
    all_to_all x1, starting transfers between devices: 9.27 us -> 6.91 us  [exchange(): return lax.all_to_all(sent, AXIS, split_axis=0, concat_axis=0)]
    pallas_call x1, Pallas kernels: 5.3 us -> 6.23 us  [own_source_rows(): pl.pallas_call(functools.partial(rows_kernel, cap), in_specs=[whole_smem(...]
    pallas_call x2 -> x3, Pallas kernels: 12.3 us -> 12.8 us  [mirror_part(): pl.pallas_call(functools.partial(mirror_part_kernel, width, masks, first)...]
    ppermute x16 -> x17, starting transfers between devices: 14.3 us -> 14.4 us  [swap(): lax.ppermute(value, AXIS, [(i, i ^ mask) for i in range(lax.axis_size(AXI...]
  transfers between devices with their start and end apart: 17 -> 18, of which waited for: 6 -> 6; matrix products, arithmetic and copies ran while one was open for 2% -> 2% of each run, Pallas kernels for 35% -> 40%
where the time goes in v1:
time: 88.7 us; the launch traced here: 87.8 us
  Pallas kernels  49.1 us (55%)
  starting transfers between devices  21.3 us (24%)
  waiting for transfers between devices  13 us (15%)
  other arithmetic  1.83 us (2%)
  between operations  1.6 us (2%)
  local copies, waits for them, and re-layouts  0.98 us (1%)
    pallas_call x6, Pallas kernels, direct_part(): pl.pallas_call(functools.partial(direct_part_kernel, width, masks, bool(m...  19 us
    ppermute x17, starting transfers between devices, swap(): lax.ppermute(value, AXIS, [(i, i ^ mask) for i in range(lax.axis_size(AXI...  14.4 us
    pallas_call x3, Pallas kernels, mirror_part(): pl.pallas_call(functools.partial(mirror_part_kernel, width, masks, first)...  12.8 us
    ppermute x17, waiting for transfers between devices, swap(): lax.ppermute(value, AXIS, [(i, i ^ mask) for i in range(lax.axis_size(AXI...  10.5 us
    pallas_call x1, Pallas kernels, own_source_cols(): pl.pallas_call(cols_kernel, grid=(width // step,), in_specs=[block, block...  10.5 us
    all_to_all x1, starting transfers between devices, exchange(): return lax.all_to_all(sent, AXIS, split_axis=0, concat_axis=0)  6.91 us
    pallas_call x1, Pallas kernels, own_source_rows(): pl.pallas_call(functools.partial(rows_kernel, cap), in_specs=[whole_smem(...  6.23 us
    all_to_all x1, waiting for transfers between devices, exchange(): return lax.all_to_all(sent, AXIS, split_axis=0, concat_axis=0)  2.44 us
  transfers between devices with their start and end apart: 18, of which 6 were waited for; matrix products, arithmetic and copies ran while one was open for 2% of the time, Pallas kernels for 40%

profile of v1, /device:TPU:0, one launch (start us, length us, event | category | flops | bytes accessed | tf_op | source)
XLA Modules:
  0.0 87.8 jit_solution(1162343784054102541)
XLA Ops:
  0.6 0.0 copy-start.1
  0.6 6.2 %own_source_rows.2 = bf16[16,32,512]{2,1,0:T(8,128)(2,1)} custom-call(s32[1]{0:T(128)} %constant.47.clone.1.round_ref, s32[1]{0:T(128)} %bitcast.1.me_ref, s32[128]{0:T(128)} %col_ref.1, bf16[512,8192]{1,0:T(8,128)(2,1)} %real_ref.21, bf16[512,8192]{1,0:T(8,128)(2,1)} %imag_ref.21), custom_call_target="tpu_custom_call" | custom-call | bytes 262144 | tf_op jit(solution)/shard_map/own_source_rows/pallas_call | solution.py:109
  6.9 6.9 %all-to-all-start.1 = ((bf16[16,32,512]{2,1,0:T(8,128)(2,1)}), bf16[16,32,512]{2,1,0:T(8,128)(2,1)S(1)}, u32[]{:S(2)}, u32[]{:S(2)}) async-start(bf16[16,32,512]{2,1,0:T(8,128)(2,1)} %own_source_rows.2), calls=%async_computation.1 | async-start | bytes 1048576 | tf_op jit(solution)/shard_map/all_to_all | solution.py:550
  13.8 0.0 copy-done.1
  13.8 0.1 convert_reduce_fusion
  13.9 0.6 reduce_max.9
  15.2 0.1 copy.9.col_ref.refs_2_
  15.3 10.5 %own_source_cols.1.refs_1_ = bf16[256,512]{1,0:T(8,128)(2,1)S(1)} custom-call(bf16[512,8192]{1,0:T(8,128)(2,1)} %real_ref.21, bf16[512,8192]{1,0:T(8,128)(2,1)} %imag_ref.21, s32[1,128]{1,0:T(1,128)S(1)} %bitcast.37), custom_call_target="tpu_custom_call" | custom-call | flops 2147483648 | bytes 16777216 | tf_op jit(solution)/shard_map/own_source_cols/pallas_call | solution.py:149
  25.8 2.4 %all-to-all-done.1.got_ref = bf16[16,32,512]{2,1,0:T(8,128)(2,1)S(1)} async-done(((bf16[16,32,512]{2,1,0:T(8,128)(2,1)}), bf16[16,32,512]{2,1,0:T(8,128)(2,1)S(1)}, u32[]{:S(2)}, u32[]{:S(2)}) %all-to-all-start.1) | async-done | bytes 524320 | tf_op jit(solution)/shard_map/all_to_all | solution.py:550
  28.3 0.6 select_rows.2
  28.8 0.0 copy-start
  28.9 0.7 copy-done
  29.5 3.7 %mirror_part.3 = (bf16[512,256]{1,0:T(8,128)(2,1)S(1)}, bf16[256,1024]{1,0:T(8,128)(2,1)S(1)}, bf16[2,256,512]{2,1,0:T(8,128)(2,1)S(1)}, f32[2,256,512]{2,1,0:T(8,128)S(1)}) custom-call(s32[1]{0:T(128)} %bitcast.1.me_ref, s32[8,8]{1,0:T(8,128)S(1)} %copy-done, bf16[512,8192]{1,0:T(8,128)(2,1)} %real_ref.21, bf16[512,8192]{1,0:T(8,128)(2,1)} %imag_ref.21, ...), custom_call_target="tpu_custom_call" | custom-call | flops 10000000000 | tf_op jit(solution)/shard_map/mirror_part/pallas_call | solution.py:393
  33.3 0.1 collective-permute-start.3
  33.3 1.2 %collective-permute-start.2 = (bf16[512,256]{1,0:T(8,128)(2,1)S(1)}, bf16[512,256]{1,0:T(8,128)(2,1)S(1)}, u32[]{:S(2)}, u32[]{:S(2)}) collective-permute-start(bf16[512,256]{1,0:T(8,128)(2,1)S(1)} %get-tuple-element.89), channel_id=1, source_target_pairs={{0,2},{1,3},{2,0},{3,1},{4,6},{5,7},{6,4},{7,5},{8,10},{9,11},{10,... | collective-permute-start | bytes 786440 | tf_op jit(solution)/shard_map/ppermute | solution.py:315
  34.5 1.2 %collective-permute-start.1 = (bf16[512,256]{1,0:T(8,128)(2,1)S(1)}, bf16[512,256]{1,0:T(8,128)(2,1)S(1)}, u32[]{:S(2)}, u32[]{:S(2)}) collective-permute-start(bf16[512,256]{1,0:T(8,128)(2,1)S(1)} %get-tuple-element.89), channel_id=1, source_target_pairs={{0,8},{1,9},{2,10},{3,11},{4,12},{5,13},{6,14},{7,15},{8,0},{9,1},... | collective-permute-start | bytes 786440 | tf_op jit(solution)/shard_map/ppermute | solution.py:315
  35.8 1.7 %collective-permute-start = (bf16[512,256]{1,0:T(8,128)(2,1)S(1)}, bf16[512,256]{1,0:T(8,128)(2,1)S(1)}, u32[]{:S(2)}, u32[]{:S(2)}) collective-permute-start(bf16[512,256]{1,0:T(8,128)(2,1)S(1)} %get-tuple-element.89), channel_id=1, source_target_pairs={{0,4},{1,5},{2,6},{3,7},{4,0},{5,1},{6,2},{7,3},{8,12},{9,13},{10,... | collective-permute-start | bytes 786440 | tf_op jit(solution)/shard_map/ppermute | solution.py:315
  37.5 0.0 collective-permute-done.3
  37.5 0.2 add_convert_fusion.1.refs_1_
  37.7 0.5 collective-permute-start.7
  38.1 3.7 %mirror_part.4 = (bf16[2,256,512]{2,1,0:T(8,128)(2,1)S(1)}, f32[2,256,512]{2,1,0:T(8,128)S(1)}) custom-call(s32[1]{0:T(128)} %bitcast.1.me_ref, s32[8,8]{1,0:T(8,128)S(1)} %copy-done, bf16[512,8192]{1,0:T(8,128)(2,1)} %real_ref.21, bf16[512,8192]{1,0:T(8,128)(2,1)} %imag_ref.21, bf16[256,1024]{1,0:T(8,128)(2,1)S(1)} %get-tuple-element.92.refs_0_, ...), custom_call_target="tpu_custom_call" | custom-call | flops 10000000000 | tf_op jit(solution)/shard_map/mirror_part/pallas_call | solution.py:393
  41.8 0.1 collective-permute-start.6
  41.9 5.4 %mirror_part.5 = (bf16[4,256,512]{2,1,0:T(8,128)(2,1)S(1)}, f32[4,256,512]{2,1,0:T(8,128)S(1)}) custom-call(s32[1]{0:T(128)} %bitcast.1.me_ref, s32[8,8]{1,0:T(8,128)S(1)} %copy-done, bf16[512,8192]{1,0:T(8,128)(2,1)} %real_ref.21, bf16[512,8192]{1,0:T(8,128)(2,1)} %imag_ref.21, bf16[256,1024]{1,0:T(8,128)(2,1)S(1)} %get-tuple-element.92.refs_0_, ...), custom_call_target="tpu_custom_call" | custom-call | flops 10000000000 | tf_op jit(solution)/shard_map/mirror_part/pallas_call | solution.py:393
  47.3 0.0 collective-permute-done.2
  47.3 1.7 %collective-permute-done.1 = bf16[512,256]{1,0:T(8,128)(2,1)S(1)} collective-permute-done((bf16[512,256]{1,0:T(8,128)(2,1)S(1)}, bf16[512,256]{1,0:T(8,128)(2,1)S(1)}, u32[]{:S(2)}, u32[]{:S(2)}) %collective-permute-start.1) | collective-permute-done | bytes 262176 | tf_op jit(solution)/shard_map/ppermute | solution.py:315
  49.0 0.0 collective-permute-done
  49.0 1.0 %collective-permute-start.4 = (bf16[512,256]{1,0:T(8,128)(2,1)S(1)}, bf16[512,256]{1,0:T(8,128)(2,1)S(1)}, u32[]{:S(2)}, u32[]{:S(2)}) collective-permute-start(bf16[512,256]{1,0:T(8,128)(2,1)S(1)} %collective-permute-done.1), channel_id=1, source_target_pairs={{0,4},{1,5},{2,6},{3,7},{4,0},{5,1},{6,2},{7,3},{8,12},{9,13},{10,... | collective-permute-start | bytes 786440 | tf_op jit(solution)/shard_map/ppermute | solution.py:315
  50.0 1.8 %collective-permute-start.9 = (bf16[512,256]{1,0:T(8,128)(2,1)S(1)}, bf16[512,256]{1,0:T(8,128)(2,1)S(1)}, u32[]{:S(2)}, u32[]{:S(2)}) collective-permute-start(bf16[512,256]{1,0:T(8,128)(2,1)S(1)} %collective-permute-done), channel_id=1, source_target_pairs={{0,2},{1,3},{2,0},{3,1},{4,6},{5,7},{6,4},{7,5},{8,10},{9,11},{10,... | collective-permute-start | bytes 786440 | tf_op jit(solution)/shard_map/ppermute | solution.py:315
  51.7 0.0 collective-permute-start.5
  51.7 1.7 %direct_part.6.refs_0_ = f32[512,256]{1,0:T(8,128)S(1)} custom-call(s32[1]{0:T(128)} %bitcast.1.me_ref, s32[8,8]{1,0:T(8,128)S(1)} %copy-done, bf16[512,8192]{1,0:T(8,128)(2,1)} %real_ref.21, bf16[512,8192]{1,0:T(8,128)(2,1)} %imag_ref.21, bf16[1,512,256]{2,1,0:T(8,128)(2,1)S(1)} %bitcast.27), custom_call_target="tpu_custom_call" | custom-call | flops 2000000000 | tf_op jit(solution)/shard_map/direct_part/pallas_call | solution.py:463
  53.5 0.3 collective-permute-done.7
  53.8 0.0 collective-permute-done.6
  53.8 0.2 convert_add_fusion.1
  54.0 1.8 %collective-permute-start.10 = (bf16[256,512]{1,0:T(8,128)(2,1)S(1)}, bf16[256,512]{1,0:T(8,128)(2,1)S(1)}, u32[]{:S(2)}, u32[]{:S(2)}) collective-permute-start(bf16[256,512]{1,0:T(8,128)(2,1)S(1)} %fusion.1), channel_id=1, source_target_pairs={{0,4},{1,5},{2,6},{3,7},{4,0},{5,1},{6,2},{7,3},{8,12},{9,13},{10,... | collective-permute-start | bytes 786440 | tf_op jit(solution)/shard_map/ppermute | solution.py:315
  55.8 0.0 collective-permute-done.5
  55.8 0.2 add_convert_fusion
  56.0 1.0 %collective-permute-start.14 = (bf16[2,256,512]{2,1,0:T(8,128)(2,1)S(1)}, bf16[2,256,512]{2,1,0:T(8,128)(2,1)S(1)}, u32[]{:S(2)}, u32[]{:S(2)}) collective-permute-start(bf16[2,256,512]{2,1,0:T(8,128)(2,1)S(1)} %add_convert_fusion), channel_id=1, source_target_pairs={{0,2},{1,3},{2,0},{3,1},{4,6},{5,7},{6,4},{7,5},{8,10},{9,11},{10,... | collective-permute-start | bytes 1572872 | tf_op jit(solution)/shard_map/ppermute | solution.py:315
  56.9 5.6 %collective-permute-done.10 = bf16[256,512]{1,0:T(8,128)(2,1)S(1)} collective-permute-done((bf16[256,512]{1,0:T(8,128)(2,1)S(1)}, bf16[256,512]{1,0:T(8,128)(2,1)S(1)}, u32[]{:S(2)}, u32[]{:S(2)}) %collective-permute-start.10) | collective-permute-done | bytes 262176 | tf_op jit(solution)/shard_map/ppermute | solution.py:315
  62.5 0.1 fusion
  62.6 1.6 %collective-permute-start.13 = (bf16[256,512]{1,0:T(8,128)(2,1)S(1)}, bf16[256,512]{1,0:T(8,128)(2,1)S(1)}, u32[]{:S(2)}, u32[]{:S(2)}) collective-permute-start(bf16[256,512]{1,0:T(8,128)(2,1)S(1)} %fusion), channel_id=1, source_target_pairs={{0,8},{1,9},{2,10},{3,11},{4,12},{5,13},{6,14},{7,15},{8,0},{9,1},... | collective-permute-start | bytes 786440 | tf_op jit(solution)/shard_map/ppermute | solution.py:315
  64.2 0.0 collective-permute-done.9
  64.2 0.0 collective-permute-done.4
  64.2 0.1 pad_maximum_fusion.1
  64.3 0.1 pad_maximum_fusion.2
  64.3 0.1 collective-permute-start.11
  64.4 1.0 %collective-permute-start.8 = (bf16[2,512,256]{2,1,0:T(8,128)(2,1)S(1)}, bf16[2,512,256]{2,1,0:T(8,128)(2,1)S(1)}, u32[]{:S(2)}, u32[]{:S(2)}) collective-permute-start(bf16[2,512,256]{2,1,0:T(8,128)(2,1)S(1)} %pad_maximum_fusion.1), channel_id=1, source_target_pairs={{0,2},{1,3},{2,0},{3,1},{4,6},{5,7},{6,4},{7,5},{8,10},{9,11},{10,... | collective-permute-start | bytes 1572872 | tf_op jit(solution)/shard_map/ppermute | solution.py:315
  65.4 0.1 pad_maximum_fusion
  65.5 0.2 collective-permute-start.12
  65.8 5.3 %direct_part.7.refs_0_ = f32[512,256]{1,0:T(8,128)S(1)} custom-call(s32[1]{0:T(128)} %bitcast.1.me_ref, s32[8,8]{1,0:T(8,128)S(1)} %copy-done, bf16[512,8192]{1,0:T(8,128)(2,1)} %real_ref.21, bf16[512,8192]{1,0:T(8,128)(2,1)} %imag_ref.21, bf16[5,512,256]{2,1,0:T(8,128)(2,1)S(1)} %constant_dynamic-update-slice_fusion.panel_ref, ...), custom_call_target="tpu_custom_call" | custom-call | flops 2000000000 | tf_op jit(solution)/shard_map/direct_part/pallas_call | solution.py:463
  71.1 0.0 collective-permute-done.14
  71.1 0.2 convert_add_fusion
  71.4 1.3 %collective-permute-start.15 = (bf16[256,512]{1,0:T(8,128)(2,1)S(1)}, bf16[256,512]{1,0:T(8,128)(2,1)S(1)}, u32[]{:S(2)}, u32[]{:S(2)}) collective-permute-start(bf16[256,512]{1,0:T(8,128)(2,1)S(1)} %fusion.2), channel_id=1, source_target_pairs={{0,4},{1,5},{2,6},{3,7},{4,0},{5,1},{6,2},{7,3},{8,12},{9,13},{10,... | collective-permute-start | bytes 786440 | tf_op jit(solution)/shard_map/ppermute | solution.py:315
  72.7 0.0 collective-permute-done.12.panel_ref
  72.7 4.1 %direct_part.8.refs_0_ = f32[512,256]{1,0:T(8,128)S(1)} custom-call(s32[1]{0:T(128)} %bitcast.1.me_ref, s32[8,8]{1,0:T(8,128)S(1)} %copy-done, bf16[512,8192]{1,0:T(8,128)(2,1)} %real_ref.21, bf16[512,8192]{1,0:T(8,128)(2,1)} %imag_ref.21, bf16[4,512,256]{2,1,0:T(8,128)(2,1)S(1)} %collective-permute-done.12.panel_ref, f32[512,256]{1,0:T(8,128)S(1)} %direct_part.7.refs_0_), custom_call_target="tpu_custom_call" | custom-call | flops 2000000000 | tf_op jit(solution)/shard_map/direct_part/pallas_call | solution.py:463
  76.9 0.0 collective-permute-done.11.panel_ref
  76.9 2.3 %direct_part.9.refs_0_ = f32[512,256]{1,0:T(8,128)S(1)} custom-call(s32[1]{0:T(128)} %bitcast.1.me_ref, s32[8,8]{1,0:T(8,128)S(1)} %copy-done, bf16[512,8192]{1,0:T(8,128)(2,1)} %real_ref.21, bf16[512,8192]{1,0:T(8,128)(2,1)} %imag_ref.21, bf16[2,512,256]{2,1,0:T(8,128)(2,1)S(1)} %collective-permute-done.11.panel_ref, f32[512,256]{1,0:T(8,128)S(1)} %direct_part.8.refs_0_), custom_call_target="tpu_custom_call" | custom-call | flops 2000000000 | tf_op jit(solution)/shard_map/direct_part/pallas_call | solution.py:463
  79.2 0.0 collective-permute-done.13.refs_1_
  79.2 2.2 %collective-permute-done.8.panel_ref = bf16[2,512,256]{2,1,0:T(8,128)(2,1)S(1)} collective-permute-done((bf16[2,512,256]{2,1,0:T(8,128)(2,1)S(1)}, bf16[2,512,256]{2,1,0:T(8,128)(2,1)S(1)}, u32[]{:S(2)}, u32[]{:S(2)}) %collective-permute-start.8) | collective-permute-done | bytes 524320 | tf_op jit(solution)/shard_map/ppermute | solution.py:315
  81.4 0.7 collective-permute-done.15.refs_3_
  82.1 0.1 collective-permute-start.16
  82.2 2.3 %direct_part.10.refs_0_ = f32[512,256]{1,0:T(8,128)S(1)} custom-call(s32[1]{0:T(128)} %bitcast.1.me_ref, s32[8,8]{1,0:T(8,128)S(1)} %copy-done, bf16[512,8192]{1,0:T(8,128)(2,1)} %real_ref.21, bf16[512,8192]{1,0:T(8,128)(2,1)} %imag_ref.21, bf16[2,512,256]{2,1,0:T(8,128)(2,1)S(1)} %collective-permute-done.8.panel_ref, f32[512,256]{1,0:T(8,128)S(1)} %direct_part.9.refs_0_), custom_call_target="tpu_custom_call" | custom-call | flops 2000000000 | tf_op jit(solution)/shard_map/direct_part/pallas_call | solution.py:463
  84.5 0.0 collective-permute-done.16.panel_ref
  84.5 3.3 %direct_part.11 = (f32[512,128]{1,0:T(8,128)}, f32[512,128]{1,0:T(8,128)}) custom-call(s32[1]{0:T(128)} %bitcast.1.me_ref, s32[8,8]{1,0:T(8,128)S(1)} %copy-done, bf16[512,8192]{1,0:T(8,128)(2,1)} %real_ref.21, bf16[512,8192]{1,0:T(8,128)(2,1)} %imag_ref.21, bf16[2,512,256]{2,1,0:T(8,128)(2,1)S(1)} %collective-permute-done.16.panel_ref, ...), custom_call_target="tpu_custom_call" | custom-call | flops 2000000000 | tf_op jit(solution)/shard_map/direct_part/pallas_call | solution.py:463
  (10 shorter events, 0.2 us)
Async XLA Ops:
  0.6 13.2 %copy-start.1 = (s32[128]{0:T(128)S(1)}, s32[128]{0:T(128)}, u32[]{:S(2)}) copy-start(s32[128]{0:T(128)} %col_ref.1) | copy-start | bytes 1540
  6.9 21.4 %all-to-all-start.1 = ((bf16[16,32,512]{2,1,0:T(8,128)(2,1)}), bf16[16,32,512]{2,1,0:T(8,128)(2,1)S(1)}, u32[]{:S(2)}, u32[]{:S(2)}) async-start(bf16[16,32,512]{2,1,0:T(8,128)(2,1)} %own_source_rows.2), calls=%async_computation.1 | async-start | bytes 1048576 | tf_op jit(solution)/shard_map/all_to_all | solution.py:550
  28.8 0.7 copy-start
  33.3 4.2 %collective-permute-start.3 = (bf16[2,256,512]{2,1,0:T(8,128)(2,1)S(1)}, bf16[2,256,512]{2,1,0:T(8,128)(2,1)S(1)}, u32[]{:S(2)}, u32[]{:S(2)}) collective-permute-start(bf16[2,256,512]{2,1,0:T(8,128)(2,1)S(1)} %get-tuple-element.91), channel_id=1, source_target_pairs={{0,1},{1,0},{2,3},{3,2},{4,5},{5,4},{6,7},{7,6},{8,9},{9,8},{10,11... | collective-permute-start | bytes 1572872 | tf_op jit(solution)/shard_map/ppermute | solution.py:315
  33.3 14.0 %collective-permute-start.2 = (bf16[512,256]{1,0:T(8,128)(2,1)S(1)}, bf16[512,256]{1,0:T(8,128)(2,1)S(1)}, u32[]{:S(2)}, u32[]{:S(2)}) collective-permute-start(bf16[512,256]{1,0:T(8,128)(2,1)S(1)} %get-tuple-element.89), channel_id=1, source_target_pairs={{0,2},{1,3},{2,0},{3,1},{4,6},{5,7},{6,4},{7,5},{8,10},{9,11},{10,... | collective-permute-start | bytes 786440 | tf_op jit(solution)/shard_map/ppermute | solution.py:315
  34.5 14.5 %collective-permute-start.1 = (bf16[512,256]{1,0:T(8,128)(2,1)S(1)}, bf16[512,256]{1,0:T(8,128)(2,1)S(1)}, u32[]{:S(2)}, u32[]{:S(2)}) collective-permute-start(bf16[512,256]{1,0:T(8,128)(2,1)S(1)} %get-tuple-element.89), channel_id=1, source_target_pairs={{0,8},{1,9},{2,10},{3,11},{4,12},{5,13},{6,14},{7,15},{8,0},{9,1},... | collective-permute-start | bytes 786440 | tf_op jit(solution)/shard_map/ppermute | solution.py:315
  35.8 13.3 %collective-permute-start = (bf16[512,256]{1,0:T(8,128)(2,1)S(1)}, bf16[512,256]{1,0:T(8,128)(2,1)S(1)}, u32[]{:S(2)}, u32[]{:S(2)}) collective-permute-start(bf16[512,256]{1,0:T(8,128)(2,1)S(1)} %get-tuple-element.89), channel_id=1, source_target_pairs={{0,4},{1,5},{2,6},{3,7},{4,0},{5,1},{6,2},{7,3},{8,12},{9,13},{10,... | collective-permute-start | bytes 786440 | tf_op jit(solution)/shard_map/ppermute | solution.py:315
  37.7 16.1 %collective-permute-start.7 = (bf16[2,256,512]{2,1,0:T(8,128)(2,1)S(1)}, bf16[2,256,512]{2,1,0:T(8,128)(2,1)S(1)}, u32[]{:S(2)}, u32[]{:S(2)}) collective-permute-start(bf16[2,256,512]{2,1,0:T(8,128)(2,1)S(1)} %add_convert_fusion.1.refs_1_), channel_id=1, source_target_pairs={{0,2},{1,3},{2,0},{3,1},{4,6},{5,7},{6,4},{7,5},{8,10},{9,11},{10,... | collective-permute-start | bytes 1572872 | tf_op jit(solution)/shard_map/ppermute | solution.py:315
  41.8 11.9 %collective-permute-start.6 = (bf16[2,256,512]{2,1,0:T(8,128)(2,1)S(1)}, bf16[2,256,512]{2,1,0:T(8,128)(2,1)S(1)}, u32[]{:S(2)}, u32[]{:S(2)}) collective-permute-start(bf16[2,256,512]{2,1,0:T(8,128)(2,1)S(1)} %get-tuple-element.99), channel_id=1, source_target_pairs={{0,1},{1,0},{2,3},{3,2},{4,5},{5,4},{6,7},{7,6},{8,9},{9,8},{10,11... | collective-permute-start | bytes 1572872 | tf_op jit(solution)/shard_map/ppermute | solution.py:315
  49.0 15.2 %collective-permute-start.4 = (bf16[512,256]{1,0:T(8,128)(2,1)S(1)}, bf16[512,256]{1,0:T(8,128)(2,1)S(1)}, u32[]{:S(2)}, u32[]{:S(2)}) collective-permute-start(bf16[512,256]{1,0:T(8,128)(2,1)S(1)} %collective-permute-done.1), channel_id=1, source_target_pairs={{0,4},{1,5},{2,6},{3,7},{4,0},{5,1},{6,2},{7,3},{8,12},{9,13},{10,... | collective-permute-start | bytes 786440 | tf_op jit(solution)/shard_map/ppermute | solution.py:315
  50.0 14.2 %collective-permute-start.9 = (bf16[512,256]{1,0:T(8,128)(2,1)S(1)}, bf16[512,256]{1,0:T(8,128)(2,1)S(1)}, u32[]{:S(2)}, u32[]{:S(2)}) collective-permute-start(bf16[512,256]{1,0:T(8,128)(2,1)S(1)} %collective-permute-done), channel_id=1, source_target_pairs={{0,2},{1,3},{2,0},{3,1},{4,6},{5,7},{6,4},{7,5},{8,10},{9,11},{10,... | collective-permute-start | bytes 786440 | tf_op jit(solution)/shard_map/ppermute | solution.py:315
  51.7 4.1 %collective-permute-start.5 = (bf16[4,256,512]{2,1,0:T(8,128)(2,1)S(1)}, bf16[4,256,512]{2,1,0:T(8,128)(2,1)S(1)}, u32[]{:S(2)}, u32[]{:S(2)}) collective-permute-start(bf16[4,256,512]{2,1,0:T(8,128)(2,1)S(1)} %get-tuple-element.98), channel_id=1, source_target_pairs={{0,1},{1,0},{2,3},{3,2},{4,5},{5,4},{6,7},{7,6},{8,9},{9,8},{10,11... | collective-permute-start | bytes 3145736 | tf_op jit(solution)/shard_map/ppermute | solution.py:315
  54.0 8.5 %collective-permute-start.10 = (bf16[256,512]{1,0:T(8,128)(2,1)S(1)}, bf16[256,512]{1,0:T(8,128)(2,1)S(1)}, u32[]{:S(2)}, u32[]{:S(2)}) collective-permute-start(bf16[256,512]{1,0:T(8,128)(2,1)S(1)} %fusion.1), channel_id=1, source_target_pairs={{0,4},{1,5},{2,6},{3,7},{4,0},{5,1},{6,2},{7,3},{8,12},{9,13},{10,... | collective-permute-start | bytes 786440 | tf_op jit(solution)/shard_map/ppermute | solution.py:315
  56.0 15.1 %collective-permute-start.14 = (bf16[2,256,512]{2,1,0:T(8,128)(2,1)S(1)}, bf16[2,256,512]{2,1,0:T(8,128)(2,1)S(1)}, u32[]{:S(2)}, u32[]{:S(2)}) collective-permute-start(bf16[2,256,512]{2,1,0:T(8,128)(2,1)S(1)} %add_convert_fusion), channel_id=1, source_target_pairs={{0,2},{1,3},{2,0},{3,1},{4,6},{5,7},{6,4},{7,5},{8,10},{9,11},{10,... | collective-permute-start | bytes 1572872 | tf_op jit(solution)/shard_map/ppermute | solution.py:315
  62.6 16.6 %collective-permute-start.13 = (bf16[256,512]{1,0:T(8,128)(2,1)S(1)}, bf16[256,512]{1,0:T(8,128)(2,1)S(1)}, u32[]{:S(2)}, u32[]{:S(2)}) collective-permute-start(bf16[256,512]{1,0:T(8,128)(2,1)S(1)} %fusion), channel_id=1, source_target_pairs={{0,8},{1,9},{2,10},{3,11},{4,12},{5,13},{6,14},{7,15},{8,0},{9,1},... | collective-permute-start | bytes 786440 | tf_op jit(solution)/shard_map/ppermute | solution.py:315
  64.3 12.5 %collective-permute-start.11 = (bf16[2,512,256]{2,1,0:T(8,128)(2,1)S(1)}, bf16[2,512,256]{2,1,0:T(8,128)(2,1)S(1)}, u32[]{:S(2)}, u32[]{:S(2)}) collective-permute-start(bf16[2,512,256]{2,1,0:T(8,128)(2,1)S(1)} %pad_maximum_fusion.2), channel_id=1, source_target_pairs={{0,1},{1,0},{2,3},{3,2},{4,5},{5,4},{6,7},{7,6},{8,9},{9,8},{10,11... | collective-permute-start | bytes 1572872 | tf_op jit(solution)/shard_map/ppermute | solution.py:315
  64.4 17.0 %collective-permute-start.8 = (bf16[2,512,256]{2,1,0:T(8,128)(2,1)S(1)}, bf16[2,512,256]{2,1,0:T(8,128)(2,1)S(1)}, u32[]{:S(2)}, u32[]{:S(2)}) collective-permute-start(bf16[2,512,256]{2,1,0:T(8,128)(2,1)S(1)} %pad_maximum_fusion.1), channel_id=1, source_target_pairs={{0,2},{1,3},{2,0},{3,1},{4,6},{5,7},{6,4},{7,5},{8,10},{9,11},{10,... | collective-permute-start | bytes 1572872 | tf_op jit(solution)/shard_map/ppermute | solution.py:315
  65.5 7.2 %collective-permute-start.12 = (bf16[4,512,256]{2,1,0:T(8,128)(2,1)S(1)}, bf16[4,512,256]{2,1,0:T(8,128)(2,1)S(1)}, u32[]{:S(2)}, u32[]{:S(2)}) collective-permute-start(bf16[4,512,256]{2,1,0:T(8,128)(2,1)S(1)} %pad_maximum_fusion), channel_id=1, source_target_pairs={{0,1},{1,0},{2,3},{3,2},{4,5},{5,4},{6,7},{7,6},{8,9},{9,8},{10,11... | collective-permute-start | bytes 3145736 | tf_op jit(solution)/shard_map/ppermute | solution.py:315
  71.4 10.7 %collective-permute-start.15 = (bf16[256,512]{1,0:T(8,128)(2,1)S(1)}, bf16[256,512]{1,0:T(8,128)(2,1)S(1)}, u32[]{:S(2)}, u32[]{:S(2)}) collective-permute-start(bf16[256,512]{1,0:T(8,128)(2,1)S(1)} %fusion.2), channel_id=1, source_target_pairs={{0,4},{1,5},{2,6},{3,7},{4,0},{5,1},{6,2},{7,3},{8,12},{9,13},{10,... | collective-permute-start | bytes 786440 | tf_op jit(solution)/shard_map/ppermute | solution.py:315
  82.1 2.4 %collective-permute-start.16 = (bf16[2,512,256]{2,1,0:T(8,128)(2,1)S(1)}, bf16[2,512,256]{2,1,0:T(8,128)(2,1)S(1)}, u32[]{:S(2)}, u32[]{:S(2)}) collective-permute-start(bf16[2,512,256]{2,1,0:T(8,128)(2,1)S(1)} %collective-permute-done.8.panel_ref), channel_id=1, source_target_pairs={{0,1},{1,0},{2,3},{3,2},{4,5},{5,4},{6,7},{7,6},{8,9},{9,8},{10,11... | collective-permute-start | bytes 1572872 | tf_op jit(solution)/shard_map/ppermute | solution.py:315

commit v2 on v1

--- a/solution.py
+++ b/solution.py
@@ -481,9 +481,10 @@
         return mirror_part(me, counts, *data, [panel_t], masks, after)
 
     far_other, far_own = part((HIGH, HIGH | LOW), [far_sent])
-    other, own = part((0, LOW, Y, Y | LOW), [far_own])
+    other, own = part((0, LOW, Y, Y | LOW), [far_own, beside])
     arrived = swap(far_sent, Y).astype(F32)
 
+    low_beside = swap(beside, LOW)
     low, high, beside = ordered([low, high, beside], [far_sent, own])
     direct = []
 
@@ -499,7 +500,7 @@
     total = total[0] + ordered(swap(to_low, LOW), [sent]).astype(F32)
     mirrors = [swap(total.astype(BF16), HIGH)]
 
-    low_beside = ordered(swap(low, Y), [sent, total])
+    low_beside = ordered(low_beside, [sent, total])
     both = ordered(swap(high, LOW), [sent, to_low])
     column = jnp.stack([panel, low, high, both])
     late = swap(ordered(jnp.stack([high, both]), [sent]), Y)

time: 88.7 us -> 95 us (1.071)
  waiting for transfers between devices: 13 us -> 19 us
    ppermute x17, waiting for transfers between devices: 10.5 us -> 16.6 us  [swap(): lax.ppermute(value, AXIS, [(i, i ^ mask) for i in range(lax.axis_size(AXI...]
  transfers between devices with their start and end apart: 18 -> 18, of which waited for: 6 -> 5; matrix products, arithmetic and copies ran while one was open for 2% -> 2% of each run, Pallas kernels for 40% -> 37%
where the time goes in v2:
time: 95 us; the launch traced here: 94.3 us
  Pallas kernels  49.1 us (52%)
  starting transfers between devices  21.8 us (23%)
  waiting for transfers between devices  19 us (20%)
  other arithmetic  1.83 us (2%)
  between operations  1.61 us (2%)
  local copies, waits for them, and re-layouts  0.98 us (1%)
    pallas_call x6, Pallas kernels, direct_part(): pl.pallas_call(functools.partial(direct_part_kernel, width, masks, bool(m...  19 us
    ppermute x17, waiting for transfers between devices, swap(): lax.ppermute(value, AXIS, [(i, i ^ mask) for i in range(lax.axis_size(AXI...  16.6 us
    ppermute x17, starting transfers between devices, swap(): lax.ppermute(value, AXIS, [(i, i ^ mask) for i in range(lax.axis_size(AXI...  14.5 us
    pallas_call x3, Pallas kernels, mirror_part(): pl.pallas_call(functools.partial(mirror_part_kernel, width, masks, first)...  12.8 us
    pallas_call x1, Pallas kernels, own_source_cols(): pl.pallas_call(cols_kernel, grid=(width // step,), in_specs=[block, block...  10.5 us
    all_to_all x1, starting transfers between devices, exchange(): return lax.all_to_all(sent, AXIS, split_axis=0, concat_axis=0)  7.31 us
    pallas_call x1, Pallas kernels, own_source_rows(): pl.pallas_call(functools.partial(rows_kernel, cap), in_specs=[whole_smem(...  6.23 us
    all_to_all x1, waiting for transfers between devices, exchange(): return lax.all_to_all(sent, AXIS, split_axis=0, concat_axis=0)  2.44 us
  transfers between devices with their start and end apart: 18, of which 5 were waited for; matrix products, arithmetic and copies ran while one was open for 2% of the time, Pallas kernels for 37%

profile of v2, /device:TPU:0, one launch (start us, length us, event | category | flops | bytes accessed | tf_op | source)
XLA Modules:
  0.0 94.3 jit_solution(14855453932341033565)
XLA Ops:
  0.6 0.0 copy-start.1
  0.6 6.2 %own_source_rows.2 = bf16[16,32,512]{2,1,0:T(8,128)(2,1)} custom-call(s32[1]{0:T(128)} %constant.47.clone.1.round_ref, s32[1]{0:T(128)} %bitcast.1.me_ref, s32[128]{0:T(128)} %col_ref.1, bf16[512,8192]{1,0:T(8,128)(2,1)} %real_ref.21, bf16[512,8192]{1,0:T(8,128)(2,1)} %imag_ref.21), custom_call_target="tpu_custom_call" | custom-call | bytes 262144 | tf_op jit(solution)/shard_map/own_source_rows/pallas_call | solution.py:109
  6.9 7.3 %all-to-all-start.1 = ((bf16[16,32,512]{2,1,0:T(8,128)(2,1)}), bf16[16,32,512]{2,1,0:T(8,128)(2,1)S(1)}, u32[]{:S(2)}, u32[]{:S(2)}) async-start(bf16[16,32,512]{2,1,0:T(8,128)(2,1)} %own_source_rows.2), calls=%async_computation.1 | async-start | bytes 1048576 | tf_op jit(solution)/shard_map/all_to_all | solution.py:551
  14.2 0.0 copy-done.1
  14.2 0.1 convert_reduce_fusion
  14.3 0.6 reduce_max.9
  15.6 0.1 copy.9.col_ref.refs_2_
  15.7 10.5 %own_source_cols.1.refs_1_ = bf16[256,512]{1,0:T(8,128)(2,1)S(1)} custom-call(bf16[512,8192]{1,0:T(8,128)(2,1)} %real_ref.21, bf16[512,8192]{1,0:T(8,128)(2,1)} %imag_ref.21, s32[1,128]{1,0:T(1,128)S(1)} %bitcast.37), custom_call_target="tpu_custom_call" | custom-call | flops 2147483648 | bytes 16777216 | tf_op jit(solution)/shard_map/own_source_cols/pallas_call | solution.py:149
  26.2 2.4 %all-to-all-done.1.got_ref = bf16[16,32,512]{2,1,0:T(8,128)(2,1)S(1)} async-done(((bf16[16,32,512]{2,1,0:T(8,128)(2,1)}), bf16[16,32,512]{2,1,0:T(8,128)(2,1)S(1)}, u32[]{:S(2)}, u32[]{:S(2)}) %all-to-all-start.1) | async-done | bytes 524320 | tf_op jit(solution)/shard_map/all_to_all | solution.py:551
  28.7 0.6 select_rows.2
  29.2 0.0 copy-start
  29.3 0.7 copy-done
  29.9 3.7 %mirror_part.3 = (bf16[512,256]{1,0:T(8,128)(2,1)S(1)}, bf16[256,1024]{1,0:T(8,128)(2,1)S(1)}, bf16[2,256,512]{2,1,0:T(8,128)(2,1)S(1)}, f32[2,256,512]{2,1,0:T(8,128)S(1)}) custom-call(s32[1]{0:T(128)} %bitcast.1.me_ref, s32[8,8]{1,0:T(8,128)S(1)} %copy-done, bf16[512,8192]{1,0:T(8,128)(2,1)} %real_ref.21, bf16[512,8192]{1,0:T(8,128)(2,1)} %imag_ref.21, ...), custom_call_target="tpu_custom_call" | custom-call | flops 10000000000 | tf_op jit(solution)/shard_map/mirror_part/pallas_call | solution.py:393
  33.7 0.1 collective-permute-start.3
  33.7 1.2 %collective-permute-start.2 = (bf16[512,256]{1,0:T(8,128)(2,1)S(1)}, bf16[512,256]{1,0:T(8,128)(2,1)S(1)}, u32[]{:S(2)}, u32[]{:S(2)}) collective-permute-start(bf16[512,256]{1,0:T(8,128)(2,1)S(1)} %get-tuple-element.89), channel_id=1, source_target_pairs={{0,2},{1,3},{2,0},{3,1},{4,6},{5,7},{6,4},{7,5},{8,10},{9,11},{10,... | collective-permute-start | bytes 786440 | tf_op jit(solution)/shard_map/ppermute | solution.py:315
  34.9 1.2 %collective-permute-start.1 = (bf16[512,256]{1,0:T(8,128)(2,1)S(1)}, bf16[512,256]{1,0:T(8,128)(2,1)S(1)}, u32[]{:S(2)}, u32[]{:S(2)}) collective-permute-start(bf16[512,256]{1,0:T(8,128)(2,1)S(1)} %get-tuple-element.89), channel_id=1, source_target_pairs={{0,8},{1,9},{2,10},{3,11},{4,12},{5,13},{6,14},{7,15},{8,0},{9,1},... | collective-permute-start | bytes 786440 | tf_op jit(solution)/shard_map/ppermute | solution.py:315
  36.1 1.7 %collective-permute-start = (bf16[512,256]{1,0:T(8,128)(2,1)S(1)}, bf16[512,256]{1,0:T(8,128)(2,1)S(1)}, u32[]{:S(2)}, u32[]{:S(2)}) collective-permute-start(bf16[512,256]{1,0:T(8,128)(2,1)S(1)} %get-tuple-element.89), channel_id=1, source_target_pairs={{0,4},{1,5},{2,6},{3,7},{4,0},{5,1},{6,2},{7,3},{8,12},{9,13},{10,... | collective-permute-start | bytes 786440 | tf_op jit(solution)/shard_map/ppermute | solution.py:315
  37.9 4.6 %collective-permute-done.2.refs_2_ = bf16[512,256]{1,0:T(8,128)(2,1)S(1)} collective-permute-done((bf16[512,256]{1,0:T(8,128)(2,1)S(1)}, bf16[512,256]{1,0:T(8,128)(2,1)S(1)}, u32[]{:S(2)}, u32[]{:S(2)}) %collective-permute-start.2) | collective-permute-done | bytes 262176 | tf_op jit(solution)/shard_map/ppermute | solution.py:315
  42.5 1.3 %collective-permute-start.9 = (bf16[512,256]{1,0:T(8,128)(2,1)S(1)}, bf16[512,256]{1,0:T(8,128)(2,1)S(1)}, u32[]{:S(2)}, u32[]{:S(2)}) collective-permute-start(bf16[512,256]{1,0:T(8,128)(2,1)S(1)} %collective-permute-done.2.refs_2_), channel_id=1, source_target_pairs={{0,4},{1,5},{2,6},{3,7},{4,0},{5,1},{6,2},{7,3},{8,12},{9,13},{10,... | collective-permute-start | bytes 786440 | tf_op jit(solution)/shard_map/ppermute | solution.py:315
  43.8 0.0 collective-permute-done.3
  43.8 0.2 add_convert_fusion.1.refs_1_
  43.9 1.1 %collective-permute-start.7 = (bf16[2,256,512]{2,1,0:T(8,128)(2,1)S(1)}, bf16[2,256,512]{2,1,0:T(8,128)(2,1)S(1)}, u32[]{:S(2)}, u32[]{:S(2)}) collective-permute-start(bf16[2,256,512]{2,1,0:T(8,128)(2,1)S(1)} %add_convert_fusion.1.refs_1_), channel_id=1, source_target_pairs={{0,2},{1,3},{2,0},{3,1},{4,6},{5,7},{6,4},{7,5},{8,10},{9,11},{10,... | collective-permute-start | bytes 1572872 | tf_op jit(solution)/shard_map/ppermute | solution.py:315
  45.1 3.7 %mirror_part.4 = (bf16[2,256,512]{2,1,0:T(8,128)(2,1)S(1)}, f32[2,256,512]{2,1,0:T(8,128)S(1)}) custom-call(s32[1]{0:T(128)} %bitcast.1.me_ref, s32[8,8]{1,0:T(8,128)S(1)} %copy-done, bf16[512,8192]{1,0:T(8,128)(2,1)} %real_ref.21, bf16[512,8192]{1,0:T(8,128)(2,1)} %imag_ref.21, bf16[256,1024]{1,0:T(8,128)(2,1)S(1)} %get-tuple-element.92.refs_0_, ...), custom_call_target="tpu_custom_call" | custom-call | flops 10000000000 | tf_op jit(solution)/shard_map/mirror_part/pallas_call | solution.py:393
  48.8 0.1 collective-permute-start.6
  48.9 5.4 %mirror_part.5 = (bf16[4,256,512]{2,1,0:T(8,128)(2,1)S(1)}, f32[4,256,512]{2,1,0:T(8,128)S(1)}) custom-call(s32[1]{0:T(128)} %bitcast.1.me_ref, s32[8,8]{1,0:T(8,128)S(1)} %copy-done, bf16[512,8192]{1,0:T(8,128)(2,1)} %real_ref.21, bf16[512,8192]{1,0:T(8,128)(2,1)} %imag_ref.21, bf16[256,1024]{1,0:T(8,128)(2,1)S(1)} %get-tuple-element.92.refs_0_, ...), custom_call_target="tpu_custom_call" | custom-call | flops 10000000000 | tf_op jit(solution)/shard_map/mirror_part/pallas_call | solution.py:393
  54.3 0.0 collective-permute-done.1
  54.3 0.0 collective-permute-done
  54.3 0.5 collective-permute-start.4
  54.7 0.2 collective-permute-start.5
  54.9 1.7 %direct_part.6.refs_0_ = f32[512,256]{1,0:T(8,128)S(1)} custom-call(s32[1]{0:T(128)} %bitcast.1.me_ref, s32[8,8]{1,0:T(8,128)S(1)} %copy-done, bf16[512,8192]{1,0:T(8,128)(2,1)} %real_ref.21, bf16[512,8192]{1,0:T(8,128)(2,1)} %imag_ref.21, bf16[1,512,256]{2,1,0:T(8,128)(2,1)S(1)} %bitcast.27), custom_call_target="tpu_custom_call" | custom-call | flops 2000000000 | tf_op jit(solution)/shard_map/direct_part/pallas_call | solution.py:463
  56.7 0.1 collective-permute-done.7
  56.8 0.0 collective-permute-done.6
  56.8 0.2 convert_add_fusion.1
  57.1 1.6 %collective-permute-start.10 = (bf16[256,512]{1,0:T(8,128)(2,1)S(1)}, bf16[256,512]{1,0:T(8,128)(2,1)S(1)}, u32[]{:S(2)}, u32[]{:S(2)}) collective-permute-start(bf16[256,512]{1,0:T(8,128)(2,1)S(1)} %fusion.1), channel_id=1, source_target_pairs={{0,4},{1,5},{2,6},{3,7},{4,0},{5,1},{6,2},{7,3},{8,12},{9,13},{10,... | collective-permute-start | bytes 786440 | tf_op jit(solution)/shard_map/ppermute | solution.py:315
  58.6 0.0 collective-permute-done.5
  58.6 0.2 add_convert_fusion
  58.8 1.0 %collective-permute-start.14 = (bf16[2,256,512]{2,1,0:T(8,128)(2,1)S(1)}, bf16[2,256,512]{2,1,0:T(8,128)(2,1)S(1)}, u32[]{:S(2)}, u32[]{:S(2)}) collective-permute-start(bf16[2,256,512]{2,1,0:T(8,128)(2,1)S(1)} %add_convert_fusion), channel_id=1, source_target_pairs={{0,2},{1,3},{2,0},{3,1},{4,6},{5,7},{6,4},{7,5},{8,10},{9,11},{10,... | collective-permute-start | bytes 1572872 | tf_op jit(solution)/shard_map/ppermute | solution.py:315
  59.9 8.8 %collective-permute-done.10 = bf16[256,512]{1,0:T(8,128)(2,1)S(1)} collective-permute-done((bf16[256,512]{1,0:T(8,128)(2,1)S(1)}, bf16[256,512]{1,0:T(8,128)(2,1)S(1)}, u32[]{:S(2)}, u32[]{:S(2)}) %collective-permute-start.10) | collective-permute-done | bytes 262176 | tf_op jit(solution)/shard_map/ppermute | solution.py:315
  68.6 0.1 fusion
  68.7 1.5 %collective-permute-start.13 = (bf16[256,512]{1,0:T(8,128)(2,1)S(1)}, bf16[256,512]{1,0:T(8,128)(2,1)S(1)}, u32[]{:S(2)}, u32[]{:S(2)}) collective-permute-start(bf16[256,512]{1,0:T(8,128)(2,1)S(1)} %fusion), channel_id=1, source_target_pairs={{0,8},{1,9},{2,10},{3,11},{4,12},{5,13},{6,14},{7,15},{8,0},{9,1},... | collective-permute-start | bytes 786440 | tf_op jit(solution)/shard_map/ppermute | solution.py:315
  70.3 0.0 collective-permute-done.9
  70.3 0.0 collective-permute-done.4
  70.3 0.1 pad_maximum_fusion.1
  70.3 0.1 pad_maximum_fusion.2
  70.4 0.1 collective-permute-start.11
  70.5 0.8 collective-permute-start.8
  71.3 0.1 pad_maximum_fusion
  71.4 0.2 collective-permute-start.12
  71.7 5.3 %direct_part.7.refs_0_ = f32[512,256]{1,0:T(8,128)S(1)} custom-call(s32[1]{0:T(128)} %bitcast.1.me_ref, s32[8,8]{1,0:T(8,128)S(1)} %copy-done, bf16[512,8192]{1,0:T(8,128)(2,1)} %real_ref.21, bf16[512,8192]{1,0:T(8,128)(2,1)} %imag_ref.21, bf16[5,512,256]{2,1,0:T(8,128)(2,1)S(1)} %constant_dynamic-update-slice_fusion.panel_ref, ...), custom_call_target="tpu_custom_call" | custom-call | flops 2000000000 | tf_op jit(solution)/shard_map/direct_part/pallas_call | solution.py:463
  77.0 0.0 collective-permute-done.14
  77.0 0.2 convert_add_fusion
  77.3 1.8 %collective-permute-start.15 = (bf16[256,512]{1,0:T(8,128)(2,1)S(1)}, bf16[256,512]{1,0:T(8,128)(2,1)S(1)}, u32[]{:S(2)}, u32[]{:S(2)}) collective-permute-start(bf16[256,512]{1,0:T(8,128)(2,1)S(1)} %fusion.2), channel_id=1, source_target_pairs={{0,4},{1,5},{2,6},{3,7},{4,0},{5,1},{6,2},{7,3},{8,12},{9,13},{10,... | collective-permute-start | bytes 786440 | tf_op jit(solution)/shard_map/ppermute | solution.py:315
  79.1 0.0 collective-permute-done.12.panel_ref
  79.1 4.1 %direct_part.8.refs_0_ = f32[512,256]{1,0:T(8,128)S(1)} custom-call(s32[1]{0:T(128)} %bitcast.1.me_ref, s32[8,8]{1,0:T(8,128)S(1)} %copy-done, bf16[512,8192]{1,0:T(8,128)(2,1)} %real_ref.21, bf16[512,8192]{1,0:T(8,128)(2,1)} %imag_ref.21, bf16[4,512,256]{2,1,0:T(8,128)(2,1)S(1)} %collective-permute-done.12.panel_ref, f32[512,256]{1,0:T(8,128)S(1)} %direct_part.7.refs_0_), custom_call_target="tpu_custom_call" | custom-call | flops 2000000000 | tf_op jit(solution)/shard_map/direct_part/pallas_call | solution.py:463
  83.3 0.0 collective-permute-done.11.panel_ref
  83.3 2.3 %direct_part.9.refs_0_ = f32[512,256]{1,0:T(8,128)S(1)} custom-call(s32[1]{0:T(128)} %bitcast.1.me_ref, s32[8,8]{1,0:T(8,128)S(1)} %copy-done, bf16[512,8192]{1,0:T(8,128)(2,1)} %real_ref.21, bf16[512,8192]{1,0:T(8,128)(2,1)} %imag_ref.21, bf16[2,512,256]{2,1,0:T(8,128)(2,1)S(1)} %collective-permute-done.11.panel_ref, f32[512,256]{1,0:T(8,128)S(1)} %direct_part.8.refs_0_), custom_call_target="tpu_custom_call" | custom-call | flops 2000000000 | tf_op jit(solution)/shard_map/direct_part/pallas_call | solution.py:463
  85.6 0.0 collective-permute-done.13.refs_1_
  85.6 0.0 collective-permute-done.8.panel_ref
  85.6 3.0 %collective-permute-done.15.refs_3_ = bf16[256,512]{1,0:T(8,128)(2,1)S(1)} collective-permute-done((bf16[256,512]{1,0:T(8,128)(2,1)S(1)}, bf16[256,512]{1,0:T(8,128)(2,1)S(1)}, u32[]{:S(2)}, u32[]{:S(2)}) %collective-permute-start.15) | collective-permute-done | bytes 262176 | tf_op jit(solution)/shard_map/ppermute | solution.py:315
  88.6 0.1 collective-permute-start.16
  88.7 2.3 %direct_part.10.refs_0_ = f32[512,256]{1,0:T(8,128)S(1)} custom-call(s32[1]{0:T(128)} %bitcast.1.me_ref, s32[8,8]{1,0:T(8,128)S(1)} %copy-done, bf16[512,8192]{1,0:T(8,128)(2,1)} %real_ref.21, bf16[512,8192]{1,0:T(8,128)(2,1)} %imag_ref.21, bf16[2,512,256]{2,1,0:T(8,128)(2,1)S(1)} %collective-permute-done.8.panel_ref, f32[512,256]{1,0:T(8,128)S(1)} %direct_part.9.refs_0_), custom_call_target="tpu_custom_call" | custom-call | flops 2000000000 | tf_op jit(solution)/shard_map/direct_part/pallas_call | solution.py:463
  91.0 0.0 collective-permute-done.16.panel_ref
  91.0 3.3 %direct_part.11 = (f32[512,128]{1,0:T(8,128)}, f32[512,128]{1,0:T(8,128)}) custom-call(s32[1]{0:T(128)} %bitcast.1.me_ref, s32[8,8]{1,0:T(8,128)S(1)} %copy-done, bf16[512,8192]{1,0:T(8,128)(2,1)} %real_ref.21, bf16[512,8192]{1,0:T(8,128)(2,1)} %imag_ref.21, bf16[2,512,256]{2,1,0:T(8,128)(2,1)S(1)} %collective-permute-done.16.panel_ref, ...), custom_call_target="tpu_custom_call" | custom-call | flops 2000000000 | tf_op jit(solution)/shard_map/direct_part/pallas_call | solution.py:463
  (10 shorter events, 0.2 us)
Async XLA Ops:
  0.6 13.6 %copy-start.1 = (s32[128]{0:T(128)S(1)}, s32[128]{0:T(128)}, u32[]{:S(2)}) copy-start(s32[128]{0:T(128)} %col_ref.1) | copy-start | bytes 1540
  6.9 21.8 %all-to-all-start.1 = ((bf16[16,32,512]{2,1,0:T(8,128)(2,1)}), bf16[16,32,512]{2,1,0:T(8,128)(2,1)S(1)}, u32[]{:S(2)}, u32[]{:S(2)}) async-start(bf16[16,32,512]{2,1,0:T(8,128)(2,1)} %own_source_rows.2), calls=%async_computation.1 | async-start | bytes 1048576 | tf_op jit(solution)/shard_map/all_to_all | solution.py:551
  29.2 0.7 copy-start
  33.7 10.1 %collective-permute-start.3 = (bf16[2,256,512]{2,1,0:T(8,128)(2,1)S(1)}, bf16[2,256,512]{2,1,0:T(8,128)(2,1)S(1)}, u32[]{:S(2)}, u32[]{:S(2)}) collective-permute-start(bf16[2,256,512]{2,1,0:T(8,128)(2,1)S(1)} %get-tuple-element.91), channel_id=1, source_target_pairs={{0,1},{1,0},{2,3},{3,2},{4,5},{5,4},{6,7},{7,6},{8,9},{9,8},{10,11... | collective-permute-start | bytes 1572872 | tf_op jit(solution)/shard_map/ppermute | solution.py:315
  33.7 8.7 %collective-permute-start.2 = (bf16[512,256]{1,0:T(8,128)(2,1)S(1)}, bf16[512,256]{1,0:T(8,128)(2,1)S(1)}, u32[]{:S(2)}, u32[]{:S(2)}) collective-permute-start(bf16[512,256]{1,0:T(8,128)(2,1)S(1)} %get-tuple-element.89), channel_id=1, source_target_pairs={{0,2},{1,3},{2,0},{3,1},{4,6},{5,7},{6,4},{7,5},{8,10},{9,11},{10,... | collective-permute-start | bytes 786440 | tf_op jit(solution)/shard_map/ppermute | solution.py:315
  34.9 19.4 %collective-permute-start.1 = (bf16[512,256]{1,0:T(8,128)(2,1)S(1)}, bf16[512,256]{1,0:T(8,128)(2,1)S(1)}, u32[]{:S(2)}, u32[]{:S(2)}) collective-permute-start(bf16[512,256]{1,0:T(8,128)(2,1)S(1)} %get-tuple-element.89), channel_id=1, source_target_pairs={{0,8},{1,9},{2,10},{3,11},{4,12},{5,13},{6,14},{7,15},{8,0},{9,1},... | collective-permute-start | bytes 786440 | tf_op jit(solution)/shard_map/ppermute | solution.py:315
  36.1 18.1 %collective-permute-start = (bf16[512,256]{1,0:T(8,128)(2,1)S(1)}, bf16[512,256]{1,0:T(8,128)(2,1)S(1)}, u32[]{:S(2)}, u32[]{:S(2)}) collective-permute-start(bf16[512,256]{1,0:T(8,128)(2,1)S(1)} %get-tuple-element.89), channel_id=1, source_target_pairs={{0,4},{1,5},{2,6},{3,7},{4,0},{5,1},{6,2},{7,3},{8,12},{9,13},{10,... | collective-permute-start | bytes 786440 | tf_op jit(solution)/shard_map/ppermute | solution.py:315
  42.5 27.8 %collective-permute-start.9 = (bf16[512,256]{1,0:T(8,128)(2,1)S(1)}, bf16[512,256]{1,0:T(8,128)(2,1)S(1)}, u32[]{:S(2)}, u32[]{:S(2)}) collective-permute-start(bf16[512,256]{1,0:T(8,128)(2,1)S(1)} %collective-permute-done.2.refs_2_), channel_id=1, source_target_pairs={{0,4},{1,5},{2,6},{3,7},{4,0},{5,1},{6,2},{7,3},{8,12},{9,13},{10,... | collective-permute-start | bytes 786440 | tf_op jit(solution)/shard_map/ppermute | solution.py:315
  43.9 12.9 %collective-permute-start.7 = (bf16[2,256,512]{2,1,0:T(8,128)(2,1)S(1)}, bf16[2,256,512]{2,1,0:T(8,128)(2,1)S(1)}, u32[]{:S(2)}, u32[]{:S(2)}) collective-permute-start(bf16[2,256,512]{2,1,0:T(8,128)(2,1)S(1)} %add_convert_fusion.1.refs_1_), channel_id=1, source_target_pairs={{0,2},{1,3},{2,0},{3,1},{4,6},{5,7},{6,4},{7,5},{8,10},{9,11},{10,... | collective-permute-start | bytes 1572872 | tf_op jit(solution)/shard_map/ppermute | solution.py:315
  48.8 8.0 %collective-permute-start.6 = (bf16[2,256,512]{2,1,0:T(8,128)(2,1)S(1)}, bf16[2,256,512]{2,1,0:T(8,128)(2,1)S(1)}, u32[]{:S(2)}, u32[]{:S(2)}) collective-permute-start(bf16[2,256,512]{2,1,0:T(8,128)(2,1)S(1)} %get-tuple-element.99), channel_id=1, source_target_pairs={{0,1},{1,0},{2,3},{3,2},{4,5},{5,4},{6,7},{7,6},{8,9},{9,8},{10,11... | collective-permute-start | bytes 1572872 | tf_op jit(solution)/shard_map/ppermute | solution.py:315
  54.3 16.0 %collective-permute-start.4 = (bf16[512,256]{1,0:T(8,128)(2,1)S(1)}, bf16[512,256]{1,0:T(8,128)(2,1)S(1)}, u32[]{:S(2)}, u32[]{:S(2)}) collective-permute-start(bf16[512,256]{1,0:T(8,128)(2,1)S(1)} %collective-permute-done.1), channel_id=1, source_target_pairs={{0,4},{1,5},{2,6},{3,7},{4,0},{5,1},{6,2},{7,3},{8,12},{9,13},{10,... | collective-permute-start | bytes 786440 | tf_op jit(solution)/shard_map/ppermute | solution.py:315
  54.7 3.9 %collective-permute-start.5 = (bf16[4,256,512]{2,1,0:T(8,128)(2,1)S(1)}, bf16[4,256,512]{2,1,0:T(8,128)(2,1)S(1)}, u32[]{:S(2)}, u32[]{:S(2)}) collective-permute-start(bf16[4,256,512]{2,1,0:T(8,128)(2,1)S(1)} %get-tuple-element.98), channel_id=1, source_target_pairs={{0,1},{1,0},{2,3},{3,2},{4,5},{5,4},{6,7},{7,6},{8,9},{9,8},{10,11... | collective-permute-start | bytes 3145736 | tf_op jit(solution)/shard_map/ppermute | solution.py:315
  57.1 11.6 %collective-permute-start.10 = (bf16[256,512]{1,0:T(8,128)(2,1)S(1)}, bf16[256,512]{1,0:T(8,128)(2,1)S(1)}, u32[]{:S(2)}, u32[]{:S(2)}) collective-permute-start(bf16[256,512]{1,0:T(8,128)(2,1)S(1)} %fusion.1), channel_id=1, source_target_pairs={{0,4},{1,5},{2,6},{3,7},{4,0},{5,1},{6,2},{7,3},{8,12},{9,13},{10,... | collective-permute-start | bytes 786440 | tf_op jit(solution)/shard_map/ppermute | solution.py:315
  58.8 18.2 %collective-permute-start.14 = (bf16[2,256,512]{2,1,0:T(8,128)(2,1)S(1)}, bf16[2,256,512]{2,1,0:T(8,128)(2,1)S(1)}, u32[]{:S(2)}, u32[]{:S(2)}) collective-permute-start(bf16[2,256,512]{2,1,0:T(8,128)(2,1)S(1)} %add_convert_fusion), channel_id=1, source_target_pairs={{0,2},{1,3},{2,0},{3,1},{4,6},{5,7},{6,4},{7,5},{8,10},{9,11},{10,... | collective-permute-start | bytes 1572872 | tf_op jit(solution)/shard_map/ppermute | solution.py:315
  68.7 16.9 %collective-permute-start.13 = (bf16[256,512]{1,0:T(8,128)(2,1)S(1)}, bf16[256,512]{1,0:T(8,128)(2,1)S(1)}, u32[]{:S(2)}, u32[]{:S(2)}) collective-permute-start(bf16[256,512]{1,0:T(8,128)(2,1)S(1)} %fusion), channel_id=1, source_target_pairs={{0,8},{1,9},{2,10},{3,11},{4,12},{5,13},{6,14},{7,15},{8,0},{9,1},... | collective-permute-start | bytes 786440 | tf_op jit(solution)/shard_map/ppermute | solution.py:315
  70.4 12.9 %collective-permute-start.11 = (bf16[2,512,256]{2,1,0:T(8,128)(2,1)S(1)}, bf16[2,512,256]{2,1,0:T(8,128)(2,1)S(1)}, u32[]{:S(2)}, u32[]{:S(2)}) collective-permute-start(bf16[2,512,256]{2,1,0:T(8,128)(2,1)S(1)} %pad_maximum_fusion.2), channel_id=1, source_target_pairs={{0,1},{1,0},{2,3},{3,2},{4,5},{5,4},{6,7},{7,6},{8,9},{9,8},{10,11... | collective-permute-start | bytes 1572872 | tf_op jit(solution)/shard_map/ppermute | solution.py:315
  70.5 15.1 %collective-permute-start.8 = (bf16[2,512,256]{2,1,0:T(8,128)(2,1)S(1)}, bf16[2,512,256]{2,1,0:T(8,128)(2,1)S(1)}, u32[]{:S(2)}, u32[]{:S(2)}) collective-permute-start(bf16[2,512,256]{2,1,0:T(8,128)(2,1)S(1)} %pad_maximum_fusion.1), channel_id=1, source_target_pairs={{0,2},{1,3},{2,0},{3,1},{4,6},{5,7},{6,4},{7,5},{8,10},{9,11},{10,... | collective-permute-start | bytes 1572872 | tf_op jit(solution)/shard_map/ppermute | solution.py:315
  71.4 7.7 %collective-permute-start.12 = (bf16[4,512,256]{2,1,0:T(8,128)(2,1)S(1)}, bf16[4,512,256]{2,1,0:T(8,128)(2,1)S(1)}, u32[]{:S(2)}, u32[]{:S(2)}) collective-permute-start(bf16[4,512,256]{2,1,0:T(8,128)(2,1)S(1)} %pad_maximum_fusion), channel_id=1, source_target_pairs={{0,1},{1,0},{2,3},{3,2},{4,5},{5,4},{6,7},{7,6},{8,9},{9,8},{10,11... | collective-permute-start | bytes 3145736 | tf_op jit(solution)/shard_map/ppermute | solution.py:315
  77.3 11.4 %collective-permute-start.15 = (bf16[256,512]{1,0:T(8,128)(2,1)S(1)}, bf16[256,512]{1,0:T(8,128)(2,1)S(1)}, u32[]{:S(2)}, u32[]{:S(2)}) collective-permute-start(bf16[256,512]{1,0:T(8,128)(2,1)S(1)} %fusion.2), channel_id=1, source_target_pairs={{0,4},{1,5},{2,6},{3,7},{4,0},{5,1},{6,2},{7,3},{8,12},{9,13},{10,... | collective-permute-start | bytes 786440 | tf_op jit(solution)/shard_map/ppermute | solution.py:315
  88.6 2.4 %collective-permute-start.16 = (bf16[2,512,256]{2,1,0:T(8,128)(2,1)S(1)}, bf16[2,512,256]{2,1,0:T(8,128)(2,1)S(1)}, u32[]{:S(2)}, u32[]{:S(2)}) collective-permute-start(bf16[2,512,256]{2,1,0:T(8,128)(2,1)S(1)} %collective-permute-done.8.panel_ref), channel_id=1, source_target_pairs={{0,1},{1,0},{2,3},{3,2},{4,5},{5,4},{6,7},{7,6},{8,9},{9,8},{10,11... | collective-permute-start | bytes 1572872 | tf_op jit(solution)/shard_map/ppermute | solution.py:315
